TPU v7x, 512 devices: a whole 4x8x8 slice. The times are simulated.
512 devices in a mesh: dp: 16 (over y, core), space: 32 (over z, x).
Axes of the slice: x: 4, y: 8, z: 8, core: 2. Of those that a mesh axis runs over, the one named last changes fastest.
Arguments:
- clips: bfloat16 [16, 1024, 9, 2, 4, 128], P('dp', 'space'), may hold values from -6 to 6
- a_tile: int32 [16, 1024], P('dp', 'space'), may hold values from 0 to 512, as said below
- gamma: float32 [128], replicated, may hold values from 0.1 to 1.9
- weight: bfloat16 [3456, 256], replicated, may hold values from -0.109375 to 0.109375
- cotangent: bfloat16 [16, 9, 32, 32, 256], P('dp', None, 'space'), may hold values from -6 to 6
Outputs:
- output: bfloat16 [16, 9, 32, 32, 256], P('dp', None, 'space')
- grad_input: bfloat16 [16, 1024, 9, 2, 4, 128], P('dp', 'space')
- grad_weight: float32 [3456, 256], P('space')
Inputs may be any that keep to these rules, and one draw needn't show every extreme that they name: `a_tile`: each of a clip's 512 tiles is held by exactly one slot; every other slot holds 512. One device's 32 slots, in every draw, hold between 8 and 32 tiles, some device all 32; among one device's tiles at most 1 have the same t // 16, and this many is reached in every draw.
All inputs are finite; a program needn't handle non-finite values.
Results may differ from a plain program's by a relative error of at most 0.0049.
Values may be sent and summed in bfloat16 or wider, within the bound.
A program may use at most 64 MiB of HBM per device.

v0:
```python
import jax
import jax.numpy as jnp
from jax import lax
from jax.sharding import PartitionSpec as P

TPD = 16


def passed_along(array, axis, by):
    count = lax.axis_size(axis)
    pairs = [(i, i + by) for i in range(count) if 0 <= i + by < count]
    return lax.ppermute(array, axis, pairs)


def activate(values, gamma):
    meansq = jnp.mean(values * values, axis=-1, keepdims=True)
    normed = values * lax.rsqrt(meansq + 1e-06) * gamma
    return jax.nn.silu(normed)


def plane(grad_taps, width):
    total = jnp.zeros((), jnp.float32)
    for frame_tap in range(3):
        for col_tap in range(3):
            piece = grad_taps[:, :, frame_tap, col_tap]
            total = total + lax.pad(
                piece,
                jnp.zeros((), piece.dtype),
                ((frame_tap, 2 - frame_tap, 0), (col_tap, 2 - col_tap, 1), (0, 0, 0)),
            )
    return total[2:, :width]


def back_taps(grad_rows, weight_part, frames, half, chans):
    product = lax.dot_general(
        grad_rows, weight_part, (((1,), (1,)), ((), ())), preferred_element_type=jnp.float32
    )
    return product.reshape(frames, half, 3, -1, 3, chans)


def send_back(slab_grad, placing, select_mat, frames, rows_in, tcols, chans, nspace, kslots):
    tile_count = placing.shape[0]
    feat = frames * rows_in * tcols * chans
    tile_grads = (
        slab_grad.reshape(frames, rows_in, tile_count, tcols, chans)
        .transpose(2, 0, 1, 3, 4)
        .reshape(tile_count, feat)
    )
    outgoing = lax.dot_general(
        placing, tile_grads, (((0,), (0,)), ((), ())), preferred_element_type=jnp.float32
    ).astype(jnp.bfloat16)
    returned = lax.all_to_all(
        outgoing.reshape(nspace, kslots, feat), "space", split_axis=0, concat_axis=0, tiled=True
    )
    slot_grads = lax.dot_general(
        select_mat,
        returned.reshape(nspace * kslots, feat),
        (((0,), (0,)), ((), ())),
        preferred_element_type=jnp.float32,
    )
    return slot_grads.astype(jnp.bfloat16)


def local(clips, a_tile, gamma, weight, cotangent):
    nspace = lax.axis_size("space")
    myself = lax.axis_index("space")
    owners = a_tile[0]
    capacity = owners.shape[0]
    kslots = capacity // nspace
    frames, rows_in, tcols, chans = clips.shape[2:]
    feat = frames * rows_in * tcols * chans
    width = TPD * tcols
    half = width // 2
    valid = owners < TPD * nspace
    dest = owners // TPD
    order = jnp.arange(capacity)
    earlier = (dest[:, None] == dest[None, :]) & (order[None, :] < order[:, None])
    rank = jnp.sum(earlier.astype(jnp.int32), axis=1)
    target = jnp.where(valid, dest * kslots + rank, -1)
    selected = target[None, :] == jnp.arange(nspace * kslots)[:, None]
    select_mat = selected.astype(jnp.bfloat16)
    sent_ids = jnp.max(jnp.where(selected, owners[None, :], -1), axis=1).reshape(nspace, kslots)
    local_x = clips[0].reshape(capacity, feat)
    moved = (
        activate(
            local_x.reshape(capacity, frames, rows_in, tcols, chans).astype(jnp.float32), gamma
        )
        .astype(jnp.bfloat16)
        .reshape(capacity, feat)
    )
    outgoing = jnp.dot(select_mat, moved, preferred_element_type=jnp.float32).astype(jnp.bfloat16)
    arrived, arrived_ids = (
        lax.all_to_all(
            outgoing.reshape(nspace, kslots, feat), "space", split_axis=0, concat_axis=0, tiled=True
        ),
        lax.all_to_all(sent_ids, "space", split_axis=0, concat_axis=0, tiled=True),
    )
    local_ids = arrived_ids.reshape(-1) - myself * TPD
    placing = (local_ids[None, :] == jnp.arange(TPD)[:, None]).astype(jnp.bfloat16)
    tiles = jnp.dot(
        placing, arrived.reshape(nspace * kslots, feat), preferred_element_type=jnp.float32
    ).astype(jnp.bfloat16)
    slab = (
        tiles.reshape(TPD, frames, rows_in, tcols, chans)
        .transpose(1, 2, 0, 3, 4)
        .reshape(frames, rows_in, width, chans)
    )
    below = passed_along(slab[:, 0], "space", -1)
    stacked = jnp.concatenate([slab, below[:, None]], axis=1)
    padded = jnp.pad(stacked, ((2, 0), (0, 0), (0, 1), (0, 0)))
    pieces = []
    for frame_tap in range(3):
        for row_tap in range(3):
            for col_tap in range(3):
                pieces.append(
                    padded[
                        frame_tap : frame_tap + frames,
                        row_tap,
                        col_tap : col_tap + 2 * half - 1 : 2,
                    ]
                )
    patches = jnp.concatenate(pieces, axis=-1).reshape(frames * half, 27 * chans)
    result = jnp.dot(patches, weight, preferred_element_type=jnp.float32).astype(jnp.bfloat16)
    output = result.reshape(1, frames, 1, half, -1)
    grad_rows = cotangent[0, :, 0].reshape(frames * half, -1)
    wrows = weight.shape[0] // nspace
    full_grad = lax.dot_general(
        patches, grad_rows, (((0,), (0,)), ((), ())), preferred_element_type=jnp.float32
    )
    summed = lax.psum(full_grad, ("dp", "space"))
    grad_weight = lax.dynamic_slice_in_dim(summed, myself * wrows, wrows, 0)
    kernel = weight.reshape(3, 3, 3, chans, -1)
    upper_kernel = kernel[:, :2].reshape(18 * chans, -1)
    lower_kernel = kernel[:, 2].reshape(9 * chans, -1)
    local_taps = back_taps(grad_rows, upper_kernel, frames, half, chans)
    first_row = plane(local_taps[:, :, :, 0], width)
    second_row = plane(local_taps[:, :, :, 1], width)
    lower_taps = back_taps(grad_rows, lower_kernel, frames, half, chans)
    rim = passed_along(plane(lower_taps[:, :, :, 0], width), "space", 1)
    grad_hidden = jnp.stack([first_row + rim, second_row], axis=1).astype(jnp.bfloat16)
    slot_grads = send_back(
        grad_hidden, placing, select_mat, frames, rows_in, tcols, chans, nspace, kslots
    )
    slot_x = local_x.reshape(capacity, frames, rows_in, tcols, chans).astype(jnp.float32)
    pull_local = jax.vjp(lambda values: activate(values, gamma), slot_x)[1]
    grad_input = pull_local(
        slot_grads.reshape(capacity, frames, rows_in, tcols, chans).astype(jnp.float32)
    )[0].astype(jnp.bfloat16)
    return (output, grad_input.reshape(1, capacity, frames, rows_in, tcols, chans), grad_weight)


def solution(mesh):
    return jax.shard_map(
        local,
        mesh=mesh,
        in_specs=(
            P("dp", "space", None, None, None, None),
            P("dp", "space"),
            P(),
            P(),
            P("dp", None, "space", None, None),
        ),
        out_specs=(
            P("dp", None, "space", None, None),
            P("dp", "space", None, None, None, None),
            P("space", None),
        ),
        check_vma=False,
    )
```

profile of v0, /device:TPU:1, one launch (start us, length us, event | category | flops | bytes accessed | tf_op | source)
XLA Modules:
  0.0 546.6 jit_solution(5011621453759333454)
XLA Ops:
  10.9 13.7 %all-to-all-start = ((s32[32,1,1]{2,1,0:T(1,128)}), s32[32,1,1]{2,1,0:T(1,128)S(1)}, u32[]{:S(2)}, u32[]{:S(2)}) async-start(s32[32,1,1]{2,1,0:T(1,128)} %copy.200), calls=%async_computation | async-start | bytes 32768 | tf_op jit(solution)/shard_map/all_to_all | solution.py:96
  26.2 3.8 pad.129
  30.0 3.7 pad.128
  36.4 3.8 collective-permute-start.1
  62.1 3.8 pad.134
  65.9 3.7 pad.133
  69.7 3.8 pad.106
  73.5 3.8 pad.104
  77.3 3.8 pad.105
  81.2 3.7 pad.142
  84.9 3.8 pad.141
  88.7 3.8 pad.140
  92.5 3.8 pad.123
  96.3 3.7 pad.122
  100.3 5.5 %pad.150 = f32[10,64,128]{2,1,0:T(8,128)} pad(f32[9,32,128]{2,1,0:T(8,128)} %get-tuple-element.57, f32[]{:T(128)} %constant.40.clone.1), padding=0_1_0x0_1_1x0_0_0 | pad | bytes 475140
  105.8 3.8 pad.149
  109.7 3.8 pad.147
  113.5 8.2 %all-to-all-start.1 = ((bf16[32,2,4608]{2,1,0:T(2,128)(2,1)}), bf16[32,2,4608]{2,1,0:T(2,128)(2,1)S(1)}, u32[]{:S(2)}, u32[]{:S(2)}) async-start(bf16[32,2,4608]{2,1,0:T(2,128)(2,1)} %reshape.206), calls=%async_computation.1 | async-start | bytes 1179648 | tf_op jit(solution)/shard_map/all_to_all | solution.py:93
  125.9 12.2 %all-to-all-done.1 = bf16[32,2,4608]{2,1,0:T(2,128)(2,1)S(1)} async-done(((bf16[32,2,4608]{2,1,0:T(2,128)(2,1)}), bf16[32,2,4608]{2,1,0:T(2,128)(2,1)S(1)}, u32[]{:S(2)}, u32[]{:S(2)}) %all-to-all-start.1) | async-done | bytes 589856 | tf_op jit(solution)/shard_map/all_to_all | solution.py:93
  143.5 7.7 %all-to-all-start.2 = ((bf16[32,2,4608]{2,1,0:T(2,128)(2,1)}), bf16[32,2,4608]{2,1,0:T(2,128)(2,1)S(1)}, u32[]{:S(2)}, u32[]{:S(2)}) async-start(bf16[32,2,4608]{2,1,0:T(2,128)(2,1)} %reshape.208), calls=%async_computation.2 | async-start | bytes 1179648 | tf_op jit(solution)/shard_map/all_to_all | solution.py:52
  151.6 3.1 slice.188
  154.6 3.0 slice.189
  257.7 3.1 fusion.29
  264.0 274.2 %all-reduce.30.cloned.1.call-done = f32[3456,256]{1,0:T(8,128)} async-done(((f32[3456,256]{1,0:T(8,128)}), f32[3456,256]{1,0:T(8,128)}) %all-reduce.30.cloned.1.call-update) | async-done | bytes 3538960 | tf_op jit(solution)/shard_map/psum | solution.py:130
  (157 shorter events, 144.5 us)
Async XLA Ops:
  7.2 17.4 %copy-start = (bf16[1,9,1,32,256]{4,3,2,1,0:T(8,128)(2,1)S(1)}, bf16[1,9,1,32,256]{4,3,2,1,0:T(8,128)(2,1)}, u32[]{:S(2)}) copy-start(bf16[1,9,1,32,256]{4,3,2,1,0:T(8,128)(2,1)} %param.9) | copy-start | bytes 442372
  10.9 102.6 %all-to-all-start = ((s32[32,1,1]{2,1,0:T(1,128)}), s32[32,1,1]{2,1,0:T(1,128)S(1)}, u32[]{:S(2)}, u32[]{:S(2)}) async-start(s32[32,1,1]{2,1,0:T(1,128)} %copy.200), calls=%async_computation | async-start | bytes 32768 | tf_op jit(solution)/shard_map/all_to_all | solution.py:96
  34.3 5.9 %copy-start.1 = (bf16[1,32,9,2,4,128]{5,4,3,2,1,0:T(4,128)(2,1)S(1)}, bf16[1,32,9,2,4,128]{5,4,3,2,1,0:T(4,128)(2,1)}, u32[]{:S(2)}) copy-start(bf16[1,32,9,2,4,128]{5,4,3,2,1,0:T(4,128)(2,1)} %param.5) | copy-start | bytes 1769476
  36.4 88.0 %collective-permute-start.1 = (f32[9,64,128]{2,1,0:T(8,128)}, f32[9,64,128]{2,1,0:T(8,128)}, u32[]{:S(2)}, u32[]{:S(2)}) collective-permute-start(f32[9,64,128]{2,1,0:T(8,128)} %fusion.47), channel_id=1, source_target_pairs={{0,1},{1,2},{2,3},{3,4},{4,5},{5,6},{6,7},{7,8},{8,9},{9,10},{10,1... | collective-permute-start | bytes 884744 | tf_op jit(solution)/shard_map/ppermute | solution.py:12
  47.1 5.3 copy-start.16
  69.7 11.5 %copy-start.13 = (f32[9,32,128]{2,1,0:T(8,128)S(1)}, f32[9,32,128]{2,1,0:T(8,128)}, u32[]{:S(2)}) copy-start(f32[9,32,128]{2,1,0:T(8,128)} %get-tuple-element.47) | copy-start | bytes 442372
  113.5 24.6 %all-to-all-start.1 = ((bf16[32,2,4608]{2,1,0:T(2,128)(2,1)}), bf16[32,2,4608]{2,1,0:T(2,128)(2,1)S(1)}, u32[]{:S(2)}, u32[]{:S(2)}) async-start(bf16[32,2,4608]{2,1,0:T(2,128)(2,1)} %reshape.206), calls=%async_computation.1 | async-start | bytes 1179648 | tf_op jit(solution)/shard_map/all_to_all | solution.py:93
  121.7 1.5 copy-start.3
  121.7 1.5 copy-start.5
  121.7 1.5 copy-start.8
  121.7 1.6 copy-start.11
  121.7 1.7 copy-start.12
  123.4 1.0 copy-start.4
  123.4 1.1 copy-start.6
  123.4 1.2 copy-start.7
  123.4 1.3 copy-start.9
  123.4 1.3 copy-start.10
  139.3 12.2 %collective-permute-start = (bf16[9,64,128]{2,1,0:T(8,128)(2,1)S(1)}, bf16[9,64,128]{2,1,0:T(8,128)(2,1)S(1)}, u32[]{:S(2)}, u32[]{:S(2)}) collective-permute-start(bf16[9,64,128]{2,1,0:T(8,128)(2,1)S(1)} %slice_bitcast_fusion.33), channel_id=1, source_target_pairs={{1,0},{2,1},{3,2},{4,3},{5,4},{6,5},{7,6},{8,7},{9,8},{10,9},{11,1... | collective-permute-start | bytes 442376 | tf_op jit(solution)/shard_map/ppermute | solution.py:12
  143.5 111.1 %all-to-all-start.2 = ((bf16[32,2,4608]{2,1,0:T(2,128)(2,1)}), bf16[32,2,4608]{2,1,0:T(2,128)(2,1)S(1)}, u32[]{:S(2)}, u32[]{:S(2)}) async-start(bf16[32,2,4608]{2,1,0:T(2,128)(2,1)} %reshape.208), calls=%async_computation.2 | async-start | bytes 1179648 | tf_op jit(solution)/shard_map/all_to_all | solution.py:52
  151.3 386.9 %all-reduce.30.cloned.1.call-start = ((), (), s32[]{:S(2)}) async-start(), calls=%async_computation.3 | async-start | bytes 7077888 | tf_op jit(solution)/shard_map/psum | solution.py:130
  227.8 20.9 %copy-start.15 = (bf16[9,1,32,128]{3,2,1,0:T(8,128)(2,1)S(1)}, bf16[9,1,32,128]{3,2,1,0:T(8,128)(2,1)}, u32[]{:S(2)}) copy-start(bf16[9,1,32,128]{3,2,1,0:T(8,128)(2,1)} %slice.211) | copy-start | bytes 221188
  227.8 21.0 %copy-start.14 = (bf16[9,1,32,128]{3,2,1,0:T(8,128)(2,1)S(1)}, bf16[9,1,32,128]{3,2,1,0:T(8,128)(2,1)}, u32[]{:S(2)}) copy-start(bf16[9,1,32,128]{3,2,1,0:T(8,128)(2,1)} %slice.212) | copy-start | bytes 221188
  256.1 1.6 copy-start.2
Sparse Core Ops, SparseCore 0:
  252.0 286.1 all-reduce.29
where the time goes:
time: 550 us; the launch traced here: 547 us
  waiting for transfers between devices  286 us (52%)
  local copies, waits for them, and re-layouts  178 us (32%)
  starting transfers between devices  35 us (6%)
  other arithmetic  20 us (4%)
  between operations  14.6 us (3%)
  matrix products  12.9 us (2%)
    psum x1, waiting for transfers between devices, local(): summed = lax.psum(full_grad, ('dp', 'space'))  274 us
    slice x27, local copies, waits for them, and re-layouts, local(): padded[frame_tap:frame_tap + frames, row_tap, col_tap:col_tap + 2 * half...  76.2 us
    unnamed x75, local copies, waits for them, and re-layouts  51 us
    slice x6, local copies, waits for them, and re-layouts, plane(): return total[2:, :width]  22.5 us
    all_to_all x1, starting transfers between devices, local(): lax.all_to_all(sent_ids, 'space', split_axis=0, concat_axis=0, tiled=True)  13.7 us
    all_to_all x1, waiting for transfers between devices, local(): lax.all_to_all(outgoing.reshape(nspace, kslots, feat), 'space', split_axi...  12.2 us
    pad x10, local copies, waits for them, and re-layouts, plane(): lax.pad(piece, jnp.zeros((), piece.dtype), ((frame_tap, 2 - frame_tap, 0)...  12.1 us
  transfers between devices with their start and end apart: 6, of which 2 were waited for; matrix products, arithmetic and copies ran while one was open for 37% of the time, Pallas kernels for 0%

commit v1 on v0

v1 whole, which is shorter than its diff:
```python
import functools

import jax
import jax.numpy as jnp
from jax import lax
from jax.experimental import pallas as pl
from jax.experimental.pallas import tpu as pltpu
from jax.sharding import PartitionSpec as P

TPD = 16
BF = jnp.bfloat16
F32 = jnp.float32
NN = (((1,), (0,)), ((), ()))
NT = (((1,), (1,)), ((), ()))
TN = (((0,), (0,)), ((), ()))


def remote(src, dst, ssem, rsem, dev):
    return pltpu.make_async_remote_copy(
        src_ref=src,
        dst_ref=dst,
        send_sem=ssem,
        recv_sem=rsem,
        device_id=dev,
        device_id_type=pl.DeviceIdType.MESH,
    )


def loop(lo, hi, body, unroll=1):
    def step(i, carry):
        body(i)
        return carry

    lax.fori_loop(lo, hi, step, 0, unroll=unroll)


def normed(x):
    meansq = jnp.mean(x * x, axis=-1, keepdims=True)
    scale = lax.rsqrt(meansq + 1e-06)
    return x * scale, scale


def kernel(
    dims,
    slot_of,
    owners,
    locs,
    clips_h,
    gamma,
    weight_h,
    cot_h,
    out,
    gin,
    fin,
    clips,
    weight,
    cot,
    cotprev,
    stage,
    arr,
    stage2,
    ret,
    locr,
    map_v,
    map_s,
    tile32,
    tiles,
    planes,
    xmat,
    gmat,
    cs,
    cr,
    cws,
    cwr,
    ccs,
    ccr,
    spst,
    spr,
    finr,
    in_sem,
    id_s,
    id_r,
    st_s,
    st_r,
    rt_s,
    rt_r,
    hop_s,
    hop_r,
    core_s,
    core_r,
    cw_s,
    cw_r,
    cc_s,
    cc_r,
    sp_s,
    sp_r,
    ag_s,
    ag_r,
):
    ns, ny, frames, half, wrows, rc = dims
    ndp = 2 * ny
    chans = 128
    tpd = half // 2
    me = lax.axis_index("space")
    dp = lax.axis_index("dp")
    y = dp // 2
    core = lax.rem(dp, 2)
    fj = frames * half

    def begin(k):
        return ((k * wrows) // 16) * 16

    loads = [
        pltpu.make_async_copy(clips_h, clips, in_sem.at[0]),
        pltpu.make_async_copy(cot_h, cot, in_sem.at[1]),
        pltpu.make_async_copy(weight_h, weight, in_sem.at[2]),
    ]
    for load in loads:
        load.start()
    barrier = pltpu.get_barrier_semaphore()

    def greet_space(i):
        pl.semaphore_signal(
            barrier,
            inc=1,
            device_id={"space": lax.rem(me + i, ns)},
            device_id_type=pl.DeviceIdType.MESH,
        )

    def greet_dp(i):
        pl.semaphore_signal(
            barrier,
            inc=1,
            device_id={"dp": lax.rem(dp + i, ndp)},
            device_id_type=pl.DeviceIdType.MESH,
        )

    loop(1, ns, greet_space)
    loop(1, ndp, greet_dp)

    @pl.when(me == 0)
    def _():
        cotprev[...] = jnp.zeros(cotprev.shape, BF)

    @pl.when(me == ns - 1)
    def _():
        xmat[:, 6 * chans : 8 * chans] = jnp.zeros((fj, 2 * chans), BF)

    gmat[:, 27 * chans :, :] = jnp.zeros((2, gmat.shape[1] - 27 * chans, 128), F32)
    gam = gamma[...]
    loads[0].wait()
    loads[1].wait()
    pl.semaphore_wait(barrier, ns - 1 + ndp - 1)

    def id_copy(d, s):
        return remote(locs.at[d], locr.at[s], id_s.at[d], id_r.at[s], {"space": d})

    def send_ids(i):
        id_copy(lax.rem(me + i, ns), me).start()

    loop(1, ns, send_ids)
    locr[me] = locs[me]

    above = lax.rem(me + ns - 1, ns)
    under = lax.rem(me + 1, ns)
    cot_copy = remote(cot, cotprev, hop_s.at[0], hop_r.at[0], {"space": under})
    row_copy = remote(
        xmat.at[:, 0 : 2 * chans],
        xmat.at[:, 6 * chans : 8 * chans],
        hop_s.at[1],
        hop_r.at[1],
        {"space": above},
    )

    @pl.when(me < ns - 1)
    def _():
        cot_copy.start()

    def hidden_of(d):
        n, _ = normed(clips[slot_of[d]].astype(F32))
        v = n * gam
        return (v / (1.0 + jnp.exp(-v))).astype(BF)

    def tile_copy(d, s):
        return remote(stage.at[d], arr.at[s], st_s.at[d], st_r.at[s], {"space": d})

    def send_tile(i):
        d = lax.rem(me + i, ns)
        stage[d] = hidden_of(d)
        tile_copy(d, me).start()

    loop(1, ns, send_tile)
    arr[me] = hidden_of(me)

    loads[2].wait()

    @pl.when(me > 0)
    def _():
        cot_copy.wait_recv()

    colrow = lax.rem(lax.broadcasted_iota(jnp.int32, (fj, chans), 0), half)

    def wpart(a, b):
        return weight[pl.ds((a * 9 + b * 3) * chans, 3 * chans), :]

    def back(source, b):
        total = lax.dot_general(source[...], wpart(2, b), NT, preferred_element_type=F32)
        for a in (1, 0):
            skip = (2 - a) * half
            part = lax.dot_general(
                source[skip:, :], wpart(a, b), NT, preferred_element_type=F32
            )
            total = total + jnp.concatenate(
                [part, jnp.zeros((skip, 3 * chans), F32)], axis=0
            )
        return total

    def put_planes(total, b):
        moved = pltpu.roll(total[:, 2 * chans :], 1, 0)
        moved = jnp.where(colrow == 0, 0.0, moved)
        planes[2 * b] = total[:, :chans] + moved
        planes[2 * b + 1] = total[:, chans : 2 * chans]

    put_planes(back(cot, 0) + back(cotprev, 2), 0)
    put_planes(back(cot, 1), 1)

    def cut_tile(t):
        for b in range(2):
            for par in range(2):
                for jj in range(2):
                    tile32[t, pl.ds(b * 4 + jj * 2 + par, frames, stride=8), :] = planes[
                        2 * b + par, pl.ds(2 * t + jj, frames, stride=half), :
                    ]
        tiles[t] = tile32[t].astype(BF)

    loop(0, tpd, cut_tile)

    def wait_id(i):
        id_copy(lax.rem(me + i, ns), lax.rem(me + i, ns)).wait_recv()

    loop(1, ns, wait_id)
    got = locr[:, 0, :]
    lane = lax.broadcasted_iota(jnp.int32, (ns, 128), 1)
    who = lax.broadcasted_iota(jnp.int32, (ns, 128), 0)
    src_of = jnp.max(jnp.where(got == lane, who, 0), axis=0, keepdims=True)
    map_v[0:ns, :] = got
    map_v[ns : ns + 8, :] = jnp.broadcast_to(src_of, (8, 128))
    to_scalar = pltpu.make_async_copy(map_v, map_s, in_sem.at[3])
    to_scalar.start()
    to_scalar.wait()

    def wait_tile(i):
        tile_copy(lax.rem(me + i, ns), lax.rem(me + i, ns)).wait_recv()

    loop(1, ns, wait_tile)

    def lay_tile(t):
        tile32[t] = arr[map_s[ns, t]].astype(F32)
        for b in range(2):
            for par in range(2):
                for jj in range(2):
                    planes[2 * b + par, pl.ds(2 * t + jj, frames, stride=half), :] = tile32[
                        t, pl.ds(b * 4 + jj * 2 + par, frames, stride=8), :
                    ]

    loop(0, tpd, lay_tile)

    def next_col(even):
        return jnp.where(colrow == half - 1, 0.0, pltpu.roll(even, fj - 1, 0)).astype(BF)

    for b in range(2):
        even = planes[2 * b]
        xmat[:, (3 * b) * chans : (3 * b + 1) * chans] = even.astype(BF)
        xmat[:, (3 * b + 1) * chans : (3 * b + 2) * chans] = planes[2 * b + 1].astype(BF)
        xmat[:, (3 * b + 2) * chans : (3 * b + 3) * chans] = next_col(even)

    @pl.when(me > 0)
    def _():
        row_copy.start()

    def back_copy(d, s):
        return remote(stage2.at[d], ret.at[s], rt_s.at[d], rt_r.at[s], {"space": d})

    def send_back(i):
        d = lax.rem(me + i, ns)
        stage2[d] = tiles[jnp.maximum(map_s[d, 0], 0)]
        back_copy(d, me).start()

    loop(1, ns, send_back)
    ret[me] = tiles[jnp.maximum(map_s[me, 0], 0)]

    def weight_grad(b):
        for a in range(3):
            count = fj - (2 - a) * half
            part = lax.dot_general(
                xmat[0:count, 3 * b * chans : 3 * (b + 1) * chans],
                cot[fj - count :, :],
                TN,
                preferred_element_type=F32,
            )
            row = (9 * a + 3 * b) * chans
            gmat[0, row : row + 3 * chans, :] = part[:, :128]
            gmat[1, row : row + 3 * chans, :] = part[:, 128:]

    weight_grad(1)
    weight_grad(0)

    @pl.when(me < ns - 1)
    def _():
        row_copy.wait_recv()

    xmat[:, 8 * chans : 9 * chans] = next_col(
        xmat[:, 6 * chans : 7 * chans].astype(F32)
    )
    weight_grad(2)

    other = {"dp": 2 * y + 1 - core}

    def core_copy(k):
        return remote(cs.at[k], cr.at[k], core_s.at[k], core_r.at[k], other)

    reach = ny // 2
    order = []
    for i in range(reach):
        order.append(reach - i)
        if i < reach - 1:
            order.append(ny - (reach - 1 - i))
    order.append(0)

    for off in order:
        k = lax.rem(y + off, ny)

        def pack(s, k=k):
            row = pl.multiple_of(begin(s) + rc * k, 16)
            cs[k, s] = gmat[1 - core, pl.ds(row, rc), :].astype(BF)

        loop(0, ns, pack)
        core_copy(k).start()

    total = lax.dot_general(xmat[...], weight[18 * chans :, :], NN, preferred_element_type=F32)
    for a in (1, 0):
        skip = (2 - a) * half
        part = lax.dot_general(
            xmat[0 : fj - skip, :],
            weight[9 * a * chans : 9 * (a + 1) * chans, :],
            NN,
            preferred_element_type=F32,
        )
        total = total + jnp.concatenate([jnp.zeros((skip, 256), F32), part], axis=0)
    out[...] = total.astype(BF)

    def mine(k, s):
        row = pl.multiple_of(begin(s) + rc * k, 16)
        return gmat[core, pl.ds(row, rc), :] + cr[k, s].astype(F32)

    up = {"dp": 2 * lax.rem(y + 1, ny) + core}
    down = {"dp": 2 * lax.rem(y + ny - 1, ny) + core}
    for i in range(reach):
        k = lax.rem(y + reach - i, ny)
        core_copy(k).wait_recv()
        if i > 0:
            remote(cws.at[i - 1], cwr.at[i - 1], cw_s.at[i - 1], cw_r.at[i - 1], up).wait_recv()

        def add_up(s, k=k, i=i):
            v = mine(k, s)
            if i > 0:
                v = v + cwr[i - 1, s].astype(F32)
            cws[i, s] = v.astype(BF)

        loop(0, ns, add_up)
        remote(cws.at[i], cwr.at[i], cw_s.at[i], cw_r.at[i], up).start()
        if i < reach - 1:
            k = lax.rem(y + ny - (reach - 1 - i), ny)
            core_copy(k).wait_recv()
            if i > 0:
                remote(
                    ccs.at[i - 1], ccr.at[i - 1], cc_s.at[i - 1], cc_r.at[i - 1], down
                ).wait_recv()

            def add_down(s, k=k, i=i):
                v = mine(k, s)
                if i > 0:
                    v = v + ccr[i - 1, s].astype(F32)
                ccs[i, s] = v.astype(BF)

            loop(0, ns, add_down)
            remote(ccs.at[i], ccr.at[i], cc_s.at[i], cc_r.at[i], down).start()

    core_copy(y).wait_recv()
    remote(
        cws.at[reach - 1], cwr.at[reach - 1], cw_s.at[reach - 1], cw_r.at[reach - 1], up
    ).wait_recv()
    if reach > 1:
        remote(
            ccs.at[reach - 2], ccr.at[reach - 2], cc_s.at[reach - 2], cc_r.at[reach - 2], down
        ).wait_recv()

    def sp_copy(d, s):
        return remote(spst.at[d], spr.at[s], sp_s.at[d], sp_r.at[s], {"space": d})

    def chunk_sum(s):
        v = mine(y, s) + cwr[reach - 1, s].astype(F32)
        if reach > 1:
            v = v + ccr[reach - 2, s].astype(F32)
        return v.astype(BF)

    def send_sp(i):
        d = lax.rem(me + i, ns)
        spst[d] = chunk_sum(d)
        sp_copy(d, me).start()

    loop(1, ns, send_sp)
    spr[me] = chunk_sum(me)

    def wait_back(i):
        back_copy(lax.rem(me + i, ns), lax.rem(me + i, ns)).wait_recv()

    loop(1, ns, wait_back)

    def pull(k):
        tile = owners[k]
        g = ret[jnp.minimum(tile // tpd, ns - 1)].astype(F32)
        g = jnp.where(tile < tpd * ns, g, 0.0)
        n, scale = normed(clips[k].astype(F32))
        v = n * gam
        sig = 1.0 / (1.0 + jnp.exp(-v))
        dn = g * sig * (1.0 + v * (1.0 - sig)) * gam
        gin[k] = (scale * (dn - n * jnp.mean(dn * n, axis=-1, keepdims=True))).astype(BF)

    loop(0, ns, pull)

    def wait_sp(i):
        sp_copy(lax.rem(me + i, ns), lax.rem(me + i, ns)).wait_recv()

    loop(1, ns, wait_sp)
    finr[core, y] = jnp.sum(spr[...].astype(F32), axis=0)

    def ag_copy(d, s):
        slot = finr.at[lax.rem(s, 2), s // 2]
        return remote(slot, slot, ag_s.at[d], ag_r.at[s], {"dp": d})

    def send_ag(i):
        ag_copy(lax.rem(dp + i, ndp), dp).start()

    loop(1, ndp, send_ag)

    def wait_ag(i):
        d = lax.rem(dp + i, ndp)
        ag_copy(d, d).wait_recv()

    loop(1, ndp, wait_ag)
    for h in range(2):
        for k in range(ny):
            fin[h, k * rc : (k + 1) * rc, :] = finr[h, k]

    def done_space(i):
        d = lax.rem(me + i, ns)
        id_copy(d, me).wait_send()
        tile_copy(d, me).wait_send()
        back_copy(d, me).wait_send()
        sp_copy(d, me).wait_send()

    loop(1, ns, done_space)

    def done_dp(i):
        ag_copy(lax.rem(dp + i, ndp), dp).wait_send()

    loop(1, ndp, done_dp)

    def done_core(k):
        core_copy(k).wait_send()

    loop(0, ny, done_core)
    for i in range(reach):
        remote(cws.at[i], cwr.at[i], cw_s.at[i], cw_r.at[i], up).wait_send()
    for i in range(reach - 1):
        remote(ccs.at[i], ccr.at[i], cc_s.at[i], cc_r.at[i], down).wait_send()

    @pl.when(me < ns - 1)
    def _():
        cot_copy.wait_send()

    @pl.when(me > 0)
    def _():
        row_copy.wait_send()


def local(clips, a_tile, gamma, weight, cotangent):
    ns = lax.axis_size("space")
    ny = lax.axis_size("dp") // 2
    me = lax.axis_index("space")
    frames, rows_in, tcols, chans = clips.shape[2:]
    half = cotangent.shape[3]
    tpd = half // 2
    cap = clips.shape[1]
    fj = frames * half
    trows = frames * rows_in * tcols
    wrows = weight.shape[0] // ns
    rc = 16 * -(-(wrows + 12) // (16 * ny))
    pad = max(((s * wrows) // 16) * 16 + rc * ny for s in range(ns))
    owners = a_tile[0]
    match = (owners // tpd)[None, :] == jnp.arange(ns)[:, None]
    slot_of = jnp.max(jnp.where(match, jnp.arange(cap)[None, :], 0), axis=1)
    col = jnp.max(jnp.where(match, (owners % tpd)[None, :], -1), axis=1)
    locs = jnp.broadcast_to(col[:, None, None], (ns, 8, 128))
    vmem = pl.BlockSpec(memory_space=pltpu.VMEM)
    smem = pl.BlockSpec(memory_space=pltpu.SMEM)
    hbm = pl.BlockSpec(memory_space=pl.ANY)
    dma = pltpu.SemaphoreType.DMA
    tiles_shape = pltpu.VMEM((ns, trows, chans), BF)
    reach = ny // 2
    piece = (ns, rc, 128)
    out, gin, fin = pl.pallas_call(
        functools.partial(kernel, (ns, ny, frames, half, wrows, rc)),
        out_shape=(
            jax.ShapeDtypeStruct((fj, 256), BF),
            jax.ShapeDtypeStruct((cap, trows, chans), BF),
            jax.ShapeDtypeStruct((2, rc * ny, 128), F32),
        ),
        in_specs=[smem, smem, vmem, hbm, vmem, hbm, hbm],
        out_specs=(vmem, vmem, vmem),
        scratch_shapes=[
            pltpu.VMEM((cap, trows, chans), BF),
            pltpu.VMEM(weight.shape, BF),
            pltpu.VMEM((fj, 256), BF),
            pltpu.VMEM((fj, 256), BF),
            tiles_shape,
            tiles_shape,
            tiles_shape,
            tiles_shape,
            pltpu.VMEM((ns, 8, 128), jnp.int32),
            pltpu.VMEM((ns + 8, 128), jnp.int32),
            pltpu.SMEM((ns + 8, 128), jnp.int32),
            pltpu.VMEM((tpd, trows, chans), F32),
            pltpu.VMEM((tpd, trows, chans), BF),
            pltpu.VMEM((4, fj, chans), F32),
            pltpu.VMEM((fj, 9 * chans), BF),
            pltpu.VMEM((2, pad, 128), F32),
            pltpu.VMEM((ny,) + piece, BF),
            pltpu.VMEM((ny,) + piece, BF),
            pltpu.VMEM((reach,) + piece, BF),
            pltpu.VMEM((reach,) + piece, BF),
            pltpu.VMEM((max(reach - 1, 1),) + piece, BF),
            pltpu.VMEM((max(reach - 1, 1),) + piece, BF),
            pltpu.VMEM(piece, BF),
            pltpu.VMEM(piece, BF),
            pltpu.VMEM((2, ny, rc, 128), F32),
            dma((4,)),
            dma((ns,)),
            dma((ns,)),
            dma((ns,)),
            dma((ns,)),
            dma((ns,)),
            dma((ns,)),
            dma((2,)),
            dma((2,)),
            dma((ny,)),
            dma((ny,)),
            dma((reach,)),
            dma((reach,)),
            dma((reach,)),
            dma((reach,)),
            dma((ns,)),
            dma((ns,)),
            dma((2 * ny,)),
            dma((2 * ny,)),
        ],
        compiler_params=pltpu.CompilerParams(
            collective_id=0, has_side_effects=True, vmem_limit_bytes=48 * 1024 * 1024
        ),
    )(
        slot_of,
        owners,
        locs,
        clips.reshape(cap, trows, chans),
        gamma.reshape(1, chans),
        weight,
        cotangent.reshape(fj, 256),
    )
    both = jnp.concatenate([fin[0], fin[1]], axis=1)
    first = me * wrows
    grad_weight = lax.dynamic_slice_in_dim(both, first - (first // 16) * 16, wrows, 0)
    return (
        out.reshape(1, frames, 1, half, 256),
        gin.reshape(clips.shape),
        grad_weight,
    )


def solution(mesh):
    return jax.shard_map(
        local,
        mesh=mesh,
        in_specs=(
            P("dp", "space", None, None, None, None),
            P("dp", "space"),
            P(),
            P(),
            P("dp", None, "space", None, None),
        ),
        out_specs=(
            P("dp", None, "space", None, None),
            P("dp", "space", None, None, None, None),
            P("space", None),
        ),
        check_vma=False,
    )
```

time: 550 us -> 102 us (0.19)
  waiting for transfers between devices: 286 us -> 0 us
  local copies, waits for them, and re-layouts: 178 us -> 6.34 us
  Pallas kernels: 0 us -> 92.9 us
  starting transfers between devices: 35 us -> 0 us
  other arithmetic: 20 us -> 1.45 us
  between operations: 14.6 us -> 0.69 us
  matrix products: 12.9 us -> 0 us
    psum x1 -> x0, waiting for transfers between devices: 274 us -> none  [local(): summed = lax.psum(full_grad, ('dp', 'space'))]
    slice x33 -> x0, local copies, waits for them, and re-layouts: 98.7 us -> none  [the longest x27 76.2 us: local(): padded[frame_tap:frame_tap + frames, row_tap, col_tap:col_tap + 2 * half...]
    pallas_call x0 -> x1, Pallas kernels: none -> 92.9 us  [local(): pl.pallas_call(functools.partial(kernel, (ns, ny, frames, half, wrows, rc...]
    unnamed x75 -> x12, local copies, waits for them, and re-layouts: 51 us -> 6.23 us
    all_to_all x3 -> x0, starting transfers between devices: 29.6 us -> none  [the longest x1 13.7 us: local(): lax.all_to_all(sent_ids, 'space', split_axis=0, concat_axis=0, tiled=True)]
    dot_general x8 -> x0, matrix products: 12.9 us -> none  [the longest x2 3.26 us: back_taps(): lax.dot_general(grad_rows, weight_part, (((1,), (1,)), ((), ())), preferr...]
    all_to_all x3 -> x0, waiting for transfers between devices: 12.2 us -> none  [the longest x1 12.2 us: local(): lax.all_to_all(outgoing.reshape(nspace, kslots, feat), 'space', split_axi...]
    pad x10 -> x0, local copies, waits for them, and re-layouts: 12.1 us -> none  [plane(): lax.pad(piece, jnp.zeros((), piece.dtype), ((frame_tap, 2 - frame_tap, 0)...]
  transfers between devices with their start and end apart: 6 -> 0, of which waited for: 2 -> 0; matrix products, arithmetic and copies ran while one was open for 37% -> 0% of each run, Pallas kernels for 0% -> 0%
where the time goes in v1:
time: 102 us; the launch traced here: 101 us
  Pallas kernels  92.9 us (91%)
  local copies, waits for them, and re-layouts  6.34 us (6%)
  other arithmetic  1.45 us (1%)
    pallas_call x1, Pallas kernels, local(): pl.pallas_call(functools.partial(kernel, (ns, ny, frames, half, wrows, rc...  92.9 us
    unnamed x12, local copies, waits for them, and re-layouts  6.23 us

profile of v1, /device:TPU:1, one launch (start us, length us, event | category | flops | bytes accessed | tf_op | source)
XLA Modules:
  0.0 101.3 jit_solution(8084897983231456232)
XLA Ops:
  0.7 0.7 fusion.2
  1.3 0.1 select_reduce_fusion
  1.4 0.1 broadcast_in_dim.37.locs
  1.5 0.0 copy-start
  1.5 1.5 %copy-done = bf16[3456,256]{1,0:T(8,128)(2,1)S(1)} copy-done((bf16[3456,256]{1,0:T(8,128)(2,1)S(1)}, bf16[3456,256]{1,0:T(8,128)(2,1)}, u32[]{:S(2)}) %copy-start) | copy-done | bytes 1769496
  3.0 0.0 copy-start.1
  3.0 1.1 %copy-done.1 = bf16[1,32,9,2,4,128]{5,4,3,2,1,0:T(4,128)(2,1)S(1)} copy-done((bf16[1,32,9,2,4,128]{5,4,3,2,1,0:T(4,128)(2,1)S(1)}, bf16[1,32,9,2,4,128]{5,4,3,2,1,0:T(4,128)(2,1)}, u32[]{:S(2)}) %copy-start.1) | copy-done | bytes 589848
  4.1 0.0 copy-start.2
  4.1 0.9 copy-done.2
  5.0 0.0 copy-start.3
  5.0 0.7 copy-done.3
  5.7 0.0 copy-start.4
  5.7 0.7 copy-done.4
  6.3 92.9 %shard_map.76 = (bf16[288,256]{1,0:T(8,128)(2,1)S(1)}, bf16[32,72,128]{2,1,0:T(8,128)(2,1)S(1)}, f32[2,128,128]{2,1,0:T(8,128)S(1)}) custom-call(s32[32]{0:T(128)S(1)} %get-tuple-element.16.slot_of, s32[32]{0:T(128)S(1)} %bitcast.20, s32[32,8,128]{2,1,0:T(8,128)S(1)} %broadcast_in_dim.37.locs, bf16[32,72,128]{2,1,0:T(8,128)(2,1)S(1)} %bitcast.17, ...), custom_call_target="tpu_custom_call" | custom-call | tf_op jit(solution)/shard_map/pallas_call | solution.py:513
  99.2 0.7 fusion
  99.9 0.7 copy.12
  100.5 0.8 copy.13
  (1 shorter events, 0.0 us)
Async XLA Ops:
  1.5 1.5 %copy-start = (bf16[3456,256]{1,0:T(8,128)(2,1)S(1)}, bf16[3456,256]{1,0:T(8,128)(2,1)}, u32[]{:S(2)}) copy-start(bf16[3456,256]{1,0:T(8,128)(2,1)} %weight_h.1) | copy-start | bytes 5308420
  3.0 1.1 %copy-start.1 = (bf16[1,32,9,2,4,128]{5,4,3,2,1,0:T(4,128)(2,1)S(1)}, bf16[1,32,9,2,4,128]{5,4,3,2,1,0:T(4,128)(2,1)}, u32[]{:S(2)}) copy-start(bf16[1,32,9,2,4,128]{5,4,3,2,1,0:T(4,128)(2,1)} %param.5) | copy-start | bytes 1769476
  4.1 0.9 copy-start.2
  5.0 0.7 copy-start.3
  5.7 0.7 copy-start.4

commit v2 on v1

v2 whole, which is shorter than its diff:
```python
import functools

import jax
import jax.numpy as jnp
from jax import lax
from jax.experimental import pallas as pl
from jax.experimental.pallas import tpu as pltpu
from jax.sharding import PartitionSpec as P

TPD = 16
BF = jnp.bfloat16
F32 = jnp.float32
NN = (((1,), (0,)), ((), ()))
NT = (((1,), (1,)), ((), ()))
TN = (((0,), (0,)), ((), ()))


def remote(src, dst, ssem, rsem, dev):
    return pltpu.make_async_remote_copy(
        src_ref=src,
        dst_ref=dst,
        send_sem=ssem,
        recv_sem=rsem,
        device_id=dev,
        device_id_type=pl.DeviceIdType.MESH,
    )


def loop(lo, hi, body, unroll=1):
    def step(i, carry):
        body(i)
        return carry

    lax.fori_loop(lo, hi, step, 0, unroll=unroll)


def normed(x):
    meansq = jnp.mean(x * x, axis=-1, keepdims=True)
    scale = lax.rsqrt(meansq + 1e-06)
    return x * scale, scale


def kernel(
    dims,
    owners,
    ids,
    clips_h,
    gamma,
    weight_h,
    cot_h,
    out,
    gin,
    fin,
    clips,
    weight,
    cot,
    cotprev,
    hid,
    slot_v,
    slot_s,
    stage,
    arr,
    stage2,
    ret,
    locr,
    map_v,
    map_s,
    tile32,
    tiles,
    planes,
    grads,
    gown,
    gtile32,
    xmat,
    gmat,
    cs,
    cr,
    cws,
    cwr,
    ccs,
    ccr,
    spst,
    spr,
    finr,
    in_sem,
    id_s,
    id_r,
    st_s,
    st_r,
    rt_s,
    rt_r,
    hop_s,
    hop_r,
    core_s,
    core_r,
    cw_s,
    cw_r,
    cc_s,
    cc_r,
    sp_s,
    sp_r,
    ag_s,
    ag_r,
):
    ns, nx, ny, frames, half, wrows, rc, flows = dims
    spans = [(f[0][0], f[-1][1]) for f in flows]
    ndp = 2 * ny
    chans = 128
    tpd = half // 2
    me = lax.axis_index("space")
    dp = lax.axis_index("dp")
    y = dp // 2
    core = lax.rem(dp, 2)
    fj = frames * half

    def begin(k):
        return ((k * wrows) // 16) * 16

    loads = [
        pltpu.make_async_copy(clips_h, clips, in_sem.at[0]),
        pltpu.make_async_copy(cot_h, cot, in_sem.at[1]),
        pltpu.make_async_copy(weight_h, weight, in_sem.at[2]),
    ]
    for load in loads:
        load.start()
    barrier = pltpu.get_barrier_semaphore()

    def greet_space(i):
        pl.semaphore_signal(
            barrier,
            inc=1,
            device_id={"space": lax.rem(me + i, ns)},
            device_id_type=pl.DeviceIdType.MESH,
        )

    def greet_dp(i):
        pl.semaphore_signal(
            barrier,
            inc=1,
            device_id={"dp": lax.rem(dp + i, ndp)},
            device_id_type=pl.DeviceIdType.MESH,
        )

    loop(1, ns, greet_space)
    loop(1, ndp, greet_dp)

    @pl.when(me == 0)
    def _():
        cotprev[...] = jnp.zeros(cotprev.shape, BF)

    @pl.when(me == ns - 1)
    def _():
        xmat[:, 6 * chans : 8 * chans] = jnp.zeros((fj, 2 * chans), BF)

    gmat[:, 27 * chans :, :] = jnp.zeros((2, gmat.shape[1] - 27 * chans, 128), F32)
    shape = (ns, 128)
    own_ids = jnp.broadcast_to(ids[...], shape)
    first_id = lax.broadcasted_iota(jnp.int32, shape, 0) * tpd
    match = (own_ids >= first_id) & (own_ids < first_id + tpd)
    slots = lax.broadcasted_iota(jnp.int32, shape, 1)
    slot_of = jnp.max(jnp.where(match, slots, 0), axis=1, keepdims=True)
    slot_of = jnp.minimum(slot_of, clips.shape[0] - 1)
    slot_v[...] = jnp.broadcast_to(slot_of, (ns, 128))
    locr[me] = ids[...]
    slot_copy = pltpu.make_async_copy(slot_v, slot_s, in_sem.at[4])
    slot_copy.start()

    gam = gamma[...]
    loads[0].wait()

    def hide(k):
        n, _ = normed(clips[k].astype(F32))
        v = n * gam
        hid[k] = (v / (1.0 + jnp.exp(-v))).astype(BF)

    loop(0, clips.shape[0], hide, 4)
    slot_copy.wait()

    def set_out(d):
        stage[d] = hid[slot_s[d, 0]]

    loop(0, ns, set_out, 4)
    arr[me] = stage[me]
    loads[1].wait()
    pl.semaphore_wait(barrier, ns - 1 + ndp - 1)

    zme = me // nx
    xme = lax.rem(me, nx)
    nz = ns // nx

    def id_x(d, s):
        return remote(
            locr.at[zme * nx + s], locr.at[zme * nx + s], id_s.at[d], id_r.at[s],
            {"space": zme * nx + d},
        )

    def id_z(d, s):
        rows = locr.at[pl.ds(s * nx, nx)]
        return remote(
            rows, rows, id_s.at[nx + d], id_r.at[nx + s], {"space": d * nx + xme}
        )

    def tile_copy(d, s):
        return remote(stage.at[d], arr.at[s], st_s.at[d], st_r.at[s], {"space": d})

    for i in range(1, nx):
        id_x(lax.rem(xme + i, nx), xme).start()

    above = lax.rem(me + ns - 1, ns)
    under = lax.rem(me + 1, ns)
    cot_copy = remote(cot, cotprev, hop_s.at[0], hop_r.at[0], {"space": under})
    row_copy = remote(
        xmat.at[:, 0 : 2 * chans],
        xmat.at[:, 6 * chans : 8 * chans],
        hop_s.at[1],
        hop_r.at[1],
        {"space": above},
    )

    def send_tile(i):
        tile_copy(lax.rem(me + i, ns), me).start()

    loop(1, ns, send_tile)

    @pl.when(me < ns - 1)
    def _():
        cot_copy.start()

    for i in range(1, nx):
        d = lax.rem(xme + i, nx)
        id_x(d, d).wait_recv()
    for i in range(1, nz):
        id_z(lax.rem(zme + i, nz), zme).start()

    loads[2].wait()
    colrow = lax.rem(lax.broadcasted_iota(jnp.int32, (fj, chans), 0), half)

    def wpart(a, b):
        return weight[pl.ds((a * 9 + b * 3) * chans, 3 * chans), :]

    def back(source, b):
        total = lax.dot_general(source[...], wpart(2, b), NT, preferred_element_type=F32)
        for a in (1, 0):
            skip = (2 - a) * half
            part = lax.dot_general(
                source[skip:, :], wpart(a, b), NT, preferred_element_type=F32
            )
            total = total + jnp.concatenate(
                [part, jnp.zeros((skip, 3 * chans), F32)], axis=0
            )
        return total

    def put_planes(total, b):
        moved = pltpu.roll(total[:, 2 * chans :], 1, 0)
        moved = jnp.where(colrow == 0, 0.0, moved)
        grads[2 * b] = total[:, :chans] + moved
        grads[2 * b + 1] = total[:, chans : 2 * chans]

    put_planes(back(cot, 1), 1)
    upper = back(cot, 0)
    gown[...] = upper

    for i in range(1, nz):
        d = lax.rem(zme + i, nz)
        id_z(d, d).wait_recv()
    every = locr[:, 0, :]
    low = me * tpd
    in_row = (every >= low) & (every < low + tpd)
    got = jnp.broadcast_to(
        jnp.max(jnp.where(in_row, every - low, -1), axis=1, keepdims=True), (ns, 128)
    )
    lane = lax.broadcasted_iota(jnp.int32, (ns, 128), 1)
    who = lax.broadcasted_iota(jnp.int32, (ns, 128), 0)
    src_of = jnp.max(jnp.where(got == lane, who, 0), axis=0, keepdims=True)
    map_v[0:ns, :] = got
    map_v[ns : ns + 8, :] = jnp.broadcast_to(src_of, (8, 128))
    to_scalar = pltpu.make_async_copy(map_v, map_s, in_sem.at[3])
    to_scalar.start()
    to_scalar.wait()

    def wait_tile(i):
        tile_copy(lax.rem(me + i, ns), lax.rem(me + i, ns)).wait_recv()

    loop(1, ns, wait_tile)

    def lay_tile(t):
        tile32[t] = arr[map_s[ns, t]].astype(F32)
        for b in range(2):
            for par in range(2):
                for jj in range(2):
                    planes[2 * b + par, pl.ds(2 * t + jj, frames, stride=half), :] = tile32[
                        t, pl.ds(b * 4 + jj * 2 + par, frames, stride=8), :
                    ]

    loop(0, tpd, lay_tile, 2)

    def next_col(even):
        return jnp.where(colrow == half - 1, 0.0, pltpu.roll(even, fj - 1, 0)).astype(BF)

    def put_rows(b):
        even = planes[2 * b]
        xmat[:, (3 * b) * chans : (3 * b + 1) * chans] = even.astype(BF)
        xmat[:, (3 * b + 1) * chans : (3 * b + 2) * chans] = planes[2 * b + 1].astype(BF)
        xmat[:, (3 * b + 2) * chans : (3 * b + 3) * chans] = next_col(even)

    put_rows(0)

    @pl.when(me > 0)
    def _():
        row_copy.start()

    put_rows(1)

    def weight_grad(b):
        for a in range(3):
            count = fj - (2 - a) * half
            part = lax.dot_general(
                xmat[0:count, 3 * b * chans : 3 * (b + 1) * chans],
                cot[fj - count :, :],
                TN,
                preferred_element_type=F32,
            )
            row = (9 * a + 3 * b) * chans
            gmat[0, row : row + 3 * chans, :] = part[:, :128]
            gmat[1, row : row + 3 * chans, :] = part[:, 128:]

    other = {"dp": 2 * y + 1 - core}

    def core_copy(k, f):
        lo, hi = spans[f]
        return remote(
            cs.at[k, lo:hi], cr.at[k, lo:hi], core_s.at[f, k], core_r.at[f, k], other
        )

    reach = ny // 2
    order = []
    for i in range(reach):
        order.append(reach - i)
        if i < reach - 1:
            order.append(ny - (reach - 1 - i))
    order.append(0)

    def each(f, body):
        for lo, hi, shift in flows[f]:
            loop(lo, hi, lambda q, shift=shift: body(q, q + shift))

    def send_core(f):
        def pack(q, s):
            row = pl.multiple_of(begin(s), 16)
            window = gmat[1 - core, pl.ds(row, rc * ny), :].astype(BF)
            cs[:, q] = window.reshape(ny, rc, 128)

        each(f, pack)
        for off in order:
            core_copy(lax.rem(y + off, ny), f).start()

    weight_grad(1)
    weight_grad(0)
    send_core(0)

    @pl.when(me > 0)
    def _():
        cot_copy.wait_recv()

    put_planes(gown[...] + back(cotprev, 2), 0)

    def cut_tile(t):
        for b in range(2):
            for par in range(2):
                for jj in range(2):
                    gtile32[t, pl.ds(b * 4 + jj * 2 + par, frames, stride=8), :] = grads[
                        2 * b + par, pl.ds(2 * t + jj, frames, stride=half), :
                    ]
        tiles[t] = gtile32[t].astype(BF)

    loop(0, tpd, cut_tile, 2)

    def back_copy(d, s):
        return remote(stage2.at[d], ret.at[s], rt_s.at[d], rt_r.at[s], {"space": d})

    def send_back(i):
        d = lax.rem(me + i, ns)
        stage2[d] = tiles[jnp.maximum(map_s[d, 0], 0)]
        back_copy(d, me).start()

    loop(1, ns, send_back)
    ret[me] = tiles[jnp.maximum(map_s[me, 0], 0)]

    @pl.when(me < ns - 1)
    def _():
        row_copy.wait_recv()

    xmat[:, 8 * chans : 9 * chans] = next_col(
        xmat[:, 6 * chans : 7 * chans].astype(F32)
    )
    weight_grad(2)
    send_core(1)

    def mine(k, q, s):
        row = pl.multiple_of(begin(s) + rc * k, 16)
        return gmat[core, pl.ds(row, rc), :] + cr[k, q].astype(F32)

    up = {"dp": 2 * lax.rem(y + 1, ny) + core}
    down = {"dp": 2 * lax.rem(y + ny - 1, ny) + core}

    def up_copy(i, f):
        lo, hi = spans[f]
        return remote(cws.at[i, lo:hi], cwr.at[i, lo:hi], cw_s.at[f, i], cw_r.at[f, i], up)

    def down_copy(i, f):
        lo, hi = spans[f]
        return remote(ccs.at[i, lo:hi], ccr.at[i, lo:hi], cc_s.at[f, i], cc_r.at[f, i], down)

    def hop(k, i, f, send, into, out_of):
        core_copy(k, f).wait_recv()
        if i > 0:
            send(i - 1, f).wait_recv()

        def add(q, s):
            v = mine(k, q, s)
            if i > 0:
                v = v + out_of[i - 1, q].astype(F32)
            into[i, q] = v.astype(BF)

        each(f, add)
        send(i, f).start()

    def chain(i):
        for f in range(2):
            hop(lax.rem(y + reach - i, ny), i, f, up_copy, cws, cwr)
            if i < reach - 1:
                hop(lax.rem(y + ny - (reach - 1 - i), ny), i, f, down_copy, ccs, ccr)

    chain(0)
    total = lax.dot_general(xmat[...], weight[18 * chans :, :], NN, preferred_element_type=F32)
    for a in (1, 0):
        skip = (2 - a) * half
        part = lax.dot_general(
            xmat[0 : fj - skip, :],
            weight[9 * a * chans : 9 * (a + 1) * chans, :],
            NN,
            preferred_element_type=F32,
        )
        total = total + jnp.concatenate([jnp.zeros((skip, 256), F32), part], axis=0)
    out[...] = total.astype(BF)

    for i in range(1, reach):
        chain(i)

    def sp_copy(d, s):
        return remote(spst.at[d], spr.at[s], sp_s.at[d], sp_r.at[s], {"space": d})

    def spread(q, s):
        v = mine(y, q, s) + cwr[reach - 1, q].astype(F32)
        if reach > 1:
            v = v + ccr[reach - 2, q].astype(F32)
        spst[s] = v.astype(BF)

        @pl.when(s != me)
        def _():
            sp_copy(s, me).start()

    for f in range(2):
        core_copy(y, f).wait_recv()
        up_copy(reach - 1, f).wait_recv()
        if reach > 1:
            down_copy(reach - 2, f).wait_recv()
        each(f, spread)
    spr[me] = spst[me]

    def wait_sp(i):
        sp_copy(lax.rem(me + i, ns), lax.rem(me + i, ns)).wait_recv()

    loop(1, ns, wait_sp)
    finr[core, y] = jnp.sum(spr[...].astype(F32), axis=0)

    def ag_copy(d, s):
        slot = finr.at[lax.rem(s, 2), s // 2]
        return remote(slot, slot, ag_s.at[d], ag_r.at[s], {"dp": d})

    def send_ag(i):
        ag_copy(lax.rem(dp + i, ndp), dp).start()

    loop(1, ndp, send_ag)

    def wait_back(i):
        back_copy(lax.rem(me + i, ns), lax.rem(me + i, ns)).wait_recv()

    loop(1, ns, wait_back)

    def pull(k):
        tile = owners[k]
        g = ret[jnp.minimum(tile // tpd, ns - 1)].astype(F32)
        g = jnp.where(tile < tpd * ns, g, 0.0)
        n, scale = normed(clips[k].astype(F32))
        v = n * gam
        sig = 1.0 / (1.0 + jnp.exp(-v))
        dn = g * sig * (1.0 + v * (1.0 - sig)) * gam
        gin[k] = (scale * (dn - n * jnp.mean(dn * n, axis=-1, keepdims=True))).astype(BF)

    loop(0, clips.shape[0], pull, 4)

    def wait_ag(i):
        d = lax.rem(dp + i, ndp)
        ag_copy(d, d).wait_recv()

    loop(1, ndp, wait_ag)
    for h in range(2):
        for k in range(ny):
            fin[h, k * rc : (k + 1) * rc, :] = finr[h, k]

    def done_space(i):
        d = lax.rem(me + i, ns)
        tile_copy(d, me).wait_send()
        back_copy(d, me).wait_send()
        sp_copy(d, me).wait_send()

    loop(1, ns, done_space)

    def done_dp(i):
        ag_copy(lax.rem(dp + i, ndp), dp).wait_send()

    loop(1, ndp, done_dp)

    for i in range(1, nx):
        id_x(lax.rem(xme + i, nx), xme).wait_send()
    for i in range(1, nz):
        id_z(lax.rem(zme + i, nz), zme).wait_send()

    def done_core(k):
        for f in range(2):
            core_copy(k, f).wait_send()

    loop(0, ny, done_core)
    for f in range(2):
        for i in range(reach):
            up_copy(i, f).wait_send()
        for i in range(reach - 1):
            down_copy(i, f).wait_send()

    @pl.when(me < ns - 1)
    def _():
        cot_copy.wait_send()

    @pl.when(me > 0)
    def _():
        row_copy.wait_send()


def flows(ns, wrows):
    kinds = [[], []]
    for s in range(ns):
        taps = range(s * wrows // 128, (s * wrows + wrows - 1) // 128 + 1)
        kinds[1 if any((tap % 9) // 3 == 2 for tap in taps) else 0].append(s)
    found = []
    q = 0
    for kind in kinds:
        ranges = []
        for s in kind:
            if ranges and ranges[-1][1] + ranges[-1][2] == s:
                ranges[-1] = (ranges[-1][0], q + 1, ranges[-1][2])
            else:
                ranges.append((q, q + 1, s - q))
            q += 1
        found.append(tuple(ranges))
    return tuple(found)


def local(clips, a_tile, gamma, weight, cotangent):
    ns = lax.axis_size("space")
    ny = lax.axis_size("dp") // 2
    me = lax.axis_index("space")
    frames, rows_in, tcols, chans = clips.shape[2:]
    half = cotangent.shape[3]
    tpd = half // 2
    cap = clips.shape[1]
    fj = frames * half
    trows = frames * rows_in * tcols
    wrows = weight.shape[0] // ns
    nx = 4
    rc = 16 * -(-(wrows + 12) // (16 * ny))
    pad = max(((s * wrows) // 16) * 16 + rc * ny for s in range(ns))
    vmem = pl.BlockSpec(memory_space=pltpu.VMEM)
    smem = pl.BlockSpec(memory_space=pltpu.SMEM)
    hbm = pl.BlockSpec(memory_space=pltpu.HBM)
    dma = pltpu.SemaphoreType.DMA
    tiles_shape = pltpu.VMEM((ns, trows, chans), BF)
    reach = ny // 2
    piece = (ns, rc, 128)
    out, gin, fin = pl.pallas_call(
        functools.partial(kernel, (ns, nx, ny, frames, half, wrows, rc, flows(ns, wrows))),
        out_shape=(
            jax.ShapeDtypeStruct((fj, 256), BF),
            jax.ShapeDtypeStruct((cap, trows, chans), BF),
            jax.ShapeDtypeStruct((2, rc * ny, 128), F32),
        ),
        in_specs=[smem, vmem, hbm, vmem, hbm, hbm],
        out_specs=(vmem, vmem, vmem),
        scratch_shapes=[
            pltpu.VMEM((cap, trows, chans), BF),
            pltpu.VMEM(weight.shape, BF),
            pltpu.VMEM((fj, 256), BF),
            pltpu.VMEM((fj, 256), BF),
            pltpu.VMEM((cap, trows, chans), BF),
            pltpu.VMEM((ns, 128), jnp.int32),
            pltpu.SMEM((ns, 128), jnp.int32),
            tiles_shape,
            tiles_shape,
            tiles_shape,
            tiles_shape,
            pltpu.VMEM((ns, 1, 128), jnp.int32),
            pltpu.VMEM((ns + 8, 128), jnp.int32),
            pltpu.SMEM((ns + 8, 128), jnp.int32),
            pltpu.VMEM((tpd, trows, chans), F32),
            pltpu.VMEM((tpd, trows, chans), BF),
            pltpu.VMEM((4, fj, chans), F32),
            pltpu.VMEM((4, fj, chans), F32),
            pltpu.VMEM((fj, 3 * chans), F32),
            pltpu.VMEM((tpd, trows, chans), F32),
            pltpu.VMEM((fj, 9 * chans), BF),
            pltpu.VMEM((2, pad, 128), F32),
            pltpu.VMEM((ny,) + piece, BF),
            pltpu.VMEM((ny,) + piece, BF),
            pltpu.VMEM((reach,) + piece, BF),
            pltpu.VMEM((reach,) + piece, BF),
            pltpu.VMEM((max(reach - 1, 1),) + piece, BF),
            pltpu.VMEM((max(reach - 1, 1),) + piece, BF),
            pltpu.VMEM(piece, BF),
            pltpu.VMEM(piece, BF),
            pltpu.VMEM((2, ny, rc, 128), F32),
            dma((5,)),
            dma((nx + ns // nx,)),
            dma((nx + ns // nx,)),
            dma((ns,)),
            dma((ns,)),
            dma((ns,)),
            dma((ns,)),
            dma((2,)),
            dma((2,)),
            dma((2, ny)),
            dma((2, ny)),
            dma((2, reach)),
            dma((2, reach)),
            dma((2, reach)),
            dma((2, reach)),
            dma((ns,)),
            dma((ns,)),
            dma((2 * ny,)),
            dma((2 * ny,)),
        ],
        compiler_params=pltpu.CompilerParams(
            collective_id=0, has_side_effects=True, vmem_limit_bytes=56 * 1024 * 1024
        ),
    )(
        a_tile[0],
        jnp.pad(a_tile, ((0, 0), (0, 128 - cap)), constant_values=tpd * ns),
        clips.reshape(cap, trows, chans),
        gamma.reshape(1, chans),
        weight,
        cotangent.reshape(fj, 256),
    )
    both = jnp.concatenate([fin[0], fin[1]], axis=1)
    first = me * wrows
    grad_weight = lax.dynamic_slice_in_dim(both, first - (first // 16) * 16, wrows, 0)
    return (
        out.reshape(1, frames, 1, half, 256),
        gin.reshape(clips.shape),
        grad_weight,
    )


def solution(mesh):
    return jax.shard_map(
        local,
        mesh=mesh,
        in_specs=(
            P("dp", "space", None, None, None, None),
            P("dp", "space"),
            P(),
            P(),
            P("dp", None, "space", None, None),
        ),
        out_specs=(
            P("dp", None, "space", None, None),
            P("dp", "space", None, None, None, None),
            P("space", None),
        ),
        check_vma=False,
    )
```

time: 102 us -> 85.2 us (0.84)
  Pallas kernels: 92.9 us -> 77.9 us
    pallas_call x1, Pallas kernels: 92.9 us -> 77.9 us  [local(): pl.pallas_call(functools.partial(kernel, (ns, nx, ny, frames, half, wrows...]
    unnamed x12 -> x2, local copies, waits for them, and re-layouts: 6.23 us -> 3.66 us
    pad x0 -> x1, local copies, waits for them, and re-layouts: none -> 1.17 us  [local(): jnp.pad(a_tile, ((0, 0), (0, 128 - cap)), constant_values=tpd * ns)]
where the time goes in v2:
time: 85.2 us; the launch traced here: 84.9 us
  Pallas kernels  77.9 us (91%)
  local copies, waits for them, and re-layouts  5.72 us (7%)
    pallas_call x1, Pallas kernels, local(): pl.pallas_call(functools.partial(kernel, (ns, nx, ny, frames, half, wrows...  77.9 us
    unnamed x2, local copies, waits for them, and re-layouts  3.66 us

profile of v2, /device:TPU:1, one launch (start us, length us, event | category | flops | bytes accessed | tf_op | source)
XLA Modules:
  0.0 84.9 jit_solution(13393436724490022166)
XLA Ops:
  0.7 1.2 %pad.4.ids = s32[1,128]{1,0:T(1,128)} pad(s32[1,32]{1,0:T(1,128)} %param.6, s32[]{:T(128)} %constant.18.clone.1), padding=0_0x0_96 | pad | bytes 644 | tf_op jit(solution)/shard_map/jit(_pad)/pad | solution.py:656
  1.8 77.9 %shard_map.76 = (bf16[288,256]{1,0:T(8,128)(2,1)}, bf16[32,72,128]{2,1,0:T(8,128)(2,1)}, f32[2,128,128]{2,1,0:T(8,128)}) custom-call(s32[32]{0:T(128)} %bitcast.16, s32[1,128]{1,0:T(1,128)} %pad.4.ids, bf16[32,72,128]{2,1,0:T(8,128)(2,1)} %bitcast.12, f32[1,128]{1,0:T(1,128)} %bitcast.17, bf16[3456,256]{1,0:T(8,128)(2,1)} %weight_h.1, bf16[288,256]{1,0:T(8,128)(2,1)} %bitcast.14), custom_call_target="tpu_custom_call" | custom-call | tf_op jit(solution)/shard_map/pallas_call | solution.py:590
  79.7 0.9 %slice_bitcast_fusion = (f32[128,128]{1,0:T(8,128)S(1)}, f32[128,128]{1,0:T(8,128)S(1)}) fusion(f32[2,128,128]{2,1,0:T(8,128)} %get-tuple-element.8), kind=kLoop, calls=%fused_computation.3 | loop fusion | bytes 262144 | tf_op jit(solution)/shard_map/squeeze | solution.py:662
  80.6 0.7 fusion
  81.2 1.6 %copy.11 = bf16[1,9,1,32,256]{4,3,2,1,0:T(8,128)(2,1)} copy(bf16[1,9,1,32,256]{4,3,2,1,0:T(8,128)(2,1)} %bitcast.15) | data formatting | bytes 294912
  82.8 2.1 %copy.12 = bf16[1,32,9,2,4,128]{5,4,3,2,1,0:T(4,128)(2,1)} copy(bf16[1,32,9,2,4,128]{5,4,3,2,1,0:T(4,128)(2,1)} %bitcast.13) | data formatting | bytes 1179648

commit v3 on v2

--- a/solution.py
+++ b/solution.py
@@ -154,14 +154,16 @@
 
     gmat[:, 27 * chans :, :] = jnp.zeros((2, gmat.shape[1] - 27 * chans, 128), F32)
     shape = (ns, 128)
-    own_ids = jnp.broadcast_to(ids[...], shape)
+    none = jnp.full((1, 128 - ids.shape[1]), tpd * ns, jnp.int32)
+    id_row = jnp.concatenate([ids[...], none], axis=1)
+    own_ids = jnp.broadcast_to(id_row, shape)
     first_id = lax.broadcasted_iota(jnp.int32, shape, 0) * tpd
     match = (own_ids >= first_id) & (own_ids < first_id + tpd)
     slots = lax.broadcasted_iota(jnp.int32, shape, 1)
     slot_of = jnp.max(jnp.where(match, slots, 0), axis=1, keepdims=True)
     slot_of = jnp.minimum(slot_of, clips.shape[0] - 1)
     slot_v[...] = jnp.broadcast_to(slot_of, (ns, 128))
-    locr[me] = ids[...]
+    locr[me] = id_row
     slot_copy = pltpu.make_async_copy(slot_v, slot_s, in_sem.at[4])
     slot_copy.start()
 
@@ -332,13 +334,8 @@
             cs.at[k, lo:hi], cr.at[k, lo:hi], core_s.at[f, k], core_r.at[f, k], other
         )
 
-    reach = ny // 2
-    order = []
-    for i in range(reach):
-        order.append(reach - i)
-        if i < reach - 1:
-            order.append(ny - (reach - 1 - i))
-    order.append(0)
+    ups = (ny // 2, ny - 1 - ny // 2)
+    downs = (ups[1], ups[0])
 
     def each(f, body):
         for lo, hi, shift in flows[f]:
@@ -351,8 +348,47 @@
             cs[:, q] = window.reshape(ny, rc, 128)
 
         each(f, pack)
-        for off in order:
-            core_copy(lax.rem(y + off, ny), f).start()
+        for i in range(max(ups[f], downs[f])):
+            if i < ups[f]:
+                core_copy(lax.rem(y + ups[f] - i, ny), f).start()
+            if i < downs[f]:
+                core_copy(lax.rem(y + ny - downs[f] + i, ny), f).start()
+        core_copy(y, f).start()
+
+    def mine(k, q, s):
+        row = pl.multiple_of(begin(s) + rc * k, 16)
+        return gmat[core, pl.ds(row, rc), :] + cr[k, q].astype(F32)
+
+    up = {"dp": 2 * lax.rem(y + 1, ny) + core}
+    down = {"dp": 2 * lax.rem(y + ny - 1, ny) + core}
+
+    def up_copy(i, f):
+        lo, hi = spans[f]
+        return remote(cws.at[i, lo:hi], cwr.at[i, lo:hi], cw_s.at[f, i], cw_r.at[f, i], up)
+
+    def down_copy(i, f):
+        lo, hi = spans[f]
+        return remote(ccs.at[i, lo:hi], ccr.at[i, lo:hi], cc_s.at[f, i], cc_r.at[f, i], down)
+
+    def hop(k, i, f, send, into, out_of):
+        core_copy(k, f).wait_recv()
+        if i > 0:
+            send(i - 1, f).wait_recv()
+
+        def add(q, s):
+            v = mine(k, q, s)
+            if i > 0:
+                v = v + out_of[i - 1, q].astype(F32)
+            into[i, q] = v.astype(BF)
+
+        each(f, add)
+        send(i, f).start()
+
+    def chain(f, i):
+        if i < ups[f]:
+            hop(lax.rem(y + ups[f] - i, ny), i, f, up_copy, cws, cwr)
+        if i < downs[f]:
+            hop(lax.rem(y + ny - downs[f] + i, ny), i, f, down_copy, ccs, ccr)
 
     weight_grad(1)
     weight_grad(0)
@@ -386,6 +422,8 @@
     loop(1, ns, send_back)
     ret[me] = tiles[jnp.maximum(map_s[me, 0], 0)]
 
+    chain(0, 0)
+
     @pl.when(me < ns - 1)
     def _():
         row_copy.wait_recv()
@@ -395,43 +433,9 @@
     )
     weight_grad(2)
     send_core(1)
-
-    def mine(k, q, s):
-        row = pl.multiple_of(begin(s) + rc * k, 16)
-        return gmat[core, pl.ds(row, rc), :] + cr[k, q].astype(F32)
-
-    up = {"dp": 2 * lax.rem(y + 1, ny) + core}
-    down = {"dp": 2 * lax.rem(y + ny - 1, ny) + core}
-
-    def up_copy(i, f):
-        lo, hi = spans[f]
-        return remote(cws.at[i, lo:hi], cwr.at[i, lo:hi], cw_s.at[f, i], cw_r.at[f, i], up)
-
-    def down_copy(i, f):
-        lo, hi = spans[f]
-        return remote(ccs.at[i, lo:hi], ccr.at[i, lo:hi], cc_s.at[f, i], cc_r.at[f, i], down)
-
-    def hop(k, i, f, send, into, out_of):
-        core_copy(k, f).wait_recv()
-        if i > 0:
-            send(i - 1, f).wait_recv()
-
-        def add(q, s):
-            v = mine(k, q, s)
-            if i > 0:
-                v = v + out_of[i - 1, q].astype(F32)
-            into[i, q] = v.astype(BF)
-
-        each(f, add)
-        send(i, f).start()
-
-    def chain(i):
-        for f in range(2):
-            hop(lax.rem(y + reach - i, ny), i, f, up_copy, cws, cwr)
-            if i < reach - 1:
-                hop(lax.rem(y + ny - (reach - 1 - i), ny), i, f, down_copy, ccs, ccr)
-
-    chain(0)
+    chain(0, 1)
+    chain(1, 0)
+
     total = lax.dot_general(xmat[...], weight[18 * chans :, :], NN, preferred_element_type=F32)
     for a in (1, 0):
         skip = (2 - a) * half
@@ -444,28 +448,36 @@
         total = total + jnp.concatenate([jnp.zeros((skip, 256), F32), part], axis=0)
     out[...] = total.astype(BF)
 
-    for i in range(1, reach):
-        chain(i)
+
+    for i in range(2, max(ups)):
+        chain(0, i)
+        chain(1, i - 1)
 
     def sp_copy(d, s):
         return remote(spst.at[d], spr.at[s], sp_s.at[d], sp_r.at[s], {"space": d})
 
-    def spread(q, s):
-        v = mine(y, q, s) + cwr[reach - 1, q].astype(F32)
-        if reach > 1:
-            v = v + ccr[reach - 2, q].astype(F32)
-        spst[s] = v.astype(BF)
-
-        @pl.when(s != me)
-        def _():
-            sp_copy(s, me).start()
-
-    for f in range(2):
+    def spread(f):
         core_copy(y, f).wait_recv()
-        up_copy(reach - 1, f).wait_recv()
-        if reach > 1:
-            down_copy(reach - 2, f).wait_recv()
-        each(f, spread)
+        for send, steps in ((up_copy, ups), (down_copy, downs)):
+            if steps[f] > 0:
+                send(steps[f] - 1, f).wait_recv()
+
+        def part(q, s):
+            v = mine(y, q, s)
+            for landed, steps in ((cwr, ups), (ccr, downs)):
+                if steps[f] > 0:
+                    v = v + landed[steps[f] - 1, q].astype(F32)
+            spst[s] = v.astype(BF)
+
+            @pl.when(s != me)
+            def _():
+                sp_copy(s, me).start()
+
+        each(f, part)
+
+    spread(0)
+    chain(1, max(ups) - 1)
+    spread(1)
     spr[me] = spst[me]
 
     def wait_sp(i):
@@ -505,9 +517,13 @@
         ag_copy(d, d).wait_recv()
 
     loop(1, ndp, wait_ag)
-    for h in range(2):
-        for k in range(ny):
-            fin[h, k * rc : (k + 1) * rc, :] = finr[h, k]
+    for off in range(0, 16, 4):
+
+        @pl.when(me * wrows - begin(me) == off)
+        def _(off=off):
+            for h in range(2):
+                window = finr[h].reshape(ny * rc, 128)
+                fin[:, h * 128 : (h + 1) * 128] = window[off : off + wrows]
 
     def done_space(i):
         d = lax.rem(me + i, ns)
@@ -533,9 +549,9 @@
 
     loop(0, ny, done_core)
     for f in range(2):
-        for i in range(reach):
+        for i in range(ups[f]):
             up_copy(i, f).wait_send()
-        for i in range(reach - 1):
+        for i in range(downs[f]):
             down_copy(i, f).wait_send()
 
     @pl.when(me < ns - 1)
@@ -545,6 +561,10 @@
     @pl.when(me > 0)
     def _():
         row_copy.wait_send()
+
+
+def pin(x):
+    return pltpu.with_memory_space_constraint(x, pltpu.HBM)
 
 
 def flows(ns, wrows):
@@ -569,7 +589,6 @@
 def local(clips, a_tile, gamma, weight, cotangent):
     ns = lax.axis_size("space")
     ny = lax.axis_size("dp") // 2
-    me = lax.axis_index("space")
     frames, rows_in, tcols, chans = clips.shape[2:]
     half = cotangent.shape[3]
     tpd = half // 2
@@ -592,7 +611,7 @@
         out_shape=(
             jax.ShapeDtypeStruct((fj, 256), BF),
             jax.ShapeDtypeStruct((cap, trows, chans), BF),
-            jax.ShapeDtypeStruct((2, rc * ny, 128), F32),
+            jax.ShapeDtypeStruct((wrows, 256), F32),
         ),
         in_specs=[smem, vmem, hbm, vmem, hbm, hbm],
         out_specs=(vmem, vmem, vmem),
@@ -623,8 +642,8 @@
             pltpu.VMEM((ny,) + piece, BF),
             pltpu.VMEM((reach,) + piece, BF),
             pltpu.VMEM((reach,) + piece, BF),
-            pltpu.VMEM((max(reach - 1, 1),) + piece, BF),
-            pltpu.VMEM((max(reach - 1, 1),) + piece, BF),
+            pltpu.VMEM((reach,) + piece, BF),
+            pltpu.VMEM((reach,) + piece, BF),
             pltpu.VMEM(piece, BF),
             pltpu.VMEM(piece, BF),
             pltpu.VMEM((2, ny, rc, 128), F32),
@@ -649,23 +668,20 @@
             dma((2 * ny,)),
         ],
         compiler_params=pltpu.CompilerParams(
-            collective_id=0, has_side_effects=True, vmem_limit_bytes=56 * 1024 * 1024
+            collective_id=0, has_side_effects=True, vmem_limit_bytes=48 * 1024 * 1024
         ),
     )(
-        a_tile[0],
-        jnp.pad(a_tile, ((0, 0), (0, 128 - cap)), constant_values=tpd * ns),
-        clips.reshape(cap, trows, chans),
-        gamma.reshape(1, chans),
-        weight,
-        cotangent.reshape(fj, 256),
+        pin(a_tile[0]),
+        pin(a_tile),
+        pin(clips.reshape(cap, trows, chans)),
+        pin(gamma.reshape(1, chans)),
+        pin(weight),
+        pin(cotangent.reshape(fj, 256)),
     )
-    both = jnp.concatenate([fin[0], fin[1]], axis=1)
-    first = me * wrows
-    grad_weight = lax.dynamic_slice_in_dim(both, first - (first // 16) * 16, wrows, 0)
     return (
         out.reshape(1, frames, 1, half, 256),
         gin.reshape(clips.shape),
-        grad_weight,
+        fin,
     )
 
 

time: 85.2 us -> 78.5 us (0.921)
  the two profiles are of different devices: /device:TPU:1 before, /device:TPU:129 now
where the time goes in v3:
time: 78.5 us; the launch traced here: 78.4 us
  Pallas kernels  75.6 us (96%)
  local copies, waits for them, and re-layouts  2.12 us (3%)
    pallas_call x1, Pallas kernels, local(): pl.pallas_call(functools.partial(kernel, (ns, nx, ny, frames, half, wrows...  75.6 us
    unnamed x3, local copies, waits for them, and re-layouts  2.12 us

profile of v3, /device:TPU:129, one launch (start us, length us, event | category | flops | bytes accessed | tf_op | source)
XLA Modules:
  0.0 78.4 jit_solution(13816456761777595278)
XLA Ops:
  0.6 75.6 %shard_map.76 = (bf16[288,256]{1,0:T(8,128)(2,1)S(1)}, bf16[32,72,128]{2,1,0:T(8,128)(2,1)S(1)}, f32[108,256]{1,0:T(8,128)S(1)}) custom-call(s32[32]{0:T(128)} %bitcast.12, s32[1,32]{1,0:T(1,128)} %ids.1, bf16[32,72,128]{2,1,0:T(8,128)(2,1)} %bitcast.10, f32[1,128]{1,0:T(1,128)} %bitcast.13, bf16[3456,256]{1,0:T(8,128)(2,1)} %weight_h.1, ...), custom_call_target="tpu_custom_call" | custom-call | tf_op jit(solution)/shard_map/pallas_call | solution.py:609
  76.3 0.7 copy.12
  76.9 0.8 %copy.13 = bf16[1,32,9,2,4,128]{5,4,3,2,1,0:T(4,128)(2,1)} copy(bf16[1,32,9,2,4,128]{5,4,3,2,1,0:T(4,128)(2,1)S(1)} %bitcast.8) | data formatting | bytes 1179648
  77.8 0.6 copy.14

commit v4 on v3

--- a/solution.py
+++ b/solution.py
@@ -101,6 +101,7 @@
     sp_r,
     ag_s,
     ag_r,
+    late_sem,
 ):
     ns, nx, ny, frames, half, wrows, rc, flows = dims
     spans = [(f[0][0], f[-1][1]) for f in flows]
@@ -133,16 +134,21 @@
             device_id_type=pl.DeviceIdType.MESH,
         )
 
-    def greet_dp(i):
+    def greet_dp(sem, j, other_core):
         pl.semaphore_signal(
-            barrier,
+            sem,
             inc=1,
-            device_id={"dp": lax.rem(dp + i, ndp)},
+            device_id={"dp": 2 * j + other_core},
             device_id_type=pl.DeviceIdType.MESH,
         )
 
+    loop(1, ny, lambda i: greet_dp(barrier, lax.rem(y + i, ny), core))
+
+    @pl.when(core == 1)
+    def _():
+        loop(0, ny, lambda j: greet_dp(barrier, j, 0))
+
     loop(1, ns, greet_space)
-    loop(1, ndp, greet_dp)
 
     @pl.when(me == 0)
     def _():
@@ -170,10 +176,12 @@
     gam = gamma[...]
     loads[0].wait()
 
+    gam_half = gam * 0.5
+
     def hide(k):
-        n, _ = normed(clips[k].astype(F32))
-        v = n * gam
-        hid[k] = (v / (1.0 + jnp.exp(-v))).astype(BF)
+        x = clips[k].astype(F32)
+        h = x * lax.rsqrt(jnp.mean(x * x, axis=-1, keepdims=True) + 1e-06) * gam_half
+        hid[k] = (h + h * jnp.tanh(h)).astype(BF)
 
     loop(0, clips.shape[0], hide, 4)
     slot_copy.wait()
@@ -184,7 +192,7 @@
     loop(0, ns, set_out, 4)
     arr[me] = stage[me]
     loads[1].wait()
-    pl.semaphore_wait(barrier, ns - 1 + ndp - 1)
+    pl.semaphore_wait(barrier, ns - 1 + ny - 1 + ny * (1 - core))
 
     zme = me // nx
     xme = lax.rem(me, nx)
@@ -227,6 +235,10 @@
     @pl.when(me < ns - 1)
     def _():
         cot_copy.start()
+
+    @pl.when(core == 0)
+    def _():
+        loop(0, ny, lambda j: greet_dp(late_sem, j, 1))
 
     for i in range(1, nx):
         d = lax.rem(xme + i, nx)
@@ -392,6 +404,11 @@
 
     weight_grad(1)
     weight_grad(0)
+
+    @pl.when(core == 1)
+    def _():
+        pl.semaphore_wait(late_sem, ny)
+
     send_core(0)
 
     @pl.when(me > 0)
@@ -411,6 +428,8 @@
 
     loop(0, tpd, cut_tile, 2)
 
+    chain(0, 0)
+
     def back_copy(d, s):
         return remote(stage2.at[d], ret.at[s], rt_s.at[d], rt_r.at[s], {"space": d})
 
@@ -421,8 +440,6 @@
 
     loop(1, ns, send_back)
     ret[me] = tiles[jnp.maximum(map_s[me, 0], 0)]
-
-    chain(0, 0)
 
     @pl.when(me < ns - 1)
     def _():
@@ -475,28 +492,42 @@
 
         each(f, part)
 
+    def done_tiles(i):
+        tile_copy(lax.rem(me + i, ns), me).wait_send()
+
+    loop(1, ns, done_tiles)
+    for i in range(1, nx):
+        id_x(lax.rem(xme + i, nx), xme).wait_send()
+    for i in range(1, nz):
+        id_z(lax.rem(zme + i, nz), zme).wait_send()
+
+    @pl.when(me < ns - 1)
+    def _():
+        cot_copy.wait_send()
+
+    @pl.when(me > 0)
+    def _():
+        row_copy.wait_send()
+
     spread(0)
     chain(1, max(ups) - 1)
     spread(1)
     spr[me] = spst[me]
 
-    def wait_sp(i):
-        sp_copy(lax.rem(me + i, ns), lax.rem(me + i, ns)).wait_recv()
-
-    loop(1, ns, wait_sp)
-    finr[core, y] = jnp.sum(spr[...].astype(F32), axis=0)
-
-    def ag_copy(d, s):
-        slot = finr.at[lax.rem(s, 2), s // 2]
-        return remote(slot, slot, ag_s.at[d], ag_r.at[s], {"dp": d})
-
-    def send_ag(i):
-        ag_copy(lax.rem(dp + i, ndp), dp).start()
-
-    loop(1, ndp, send_ag)
+    def done_core(k):
+        for f in range(2):
+            core_copy(k, f).wait_send()
+
+    loop(0, ny, done_core)
+    for f in range(2):
+        for i in range(ups[f]):
+            up_copy(i, f).wait_send()
+        for i in range(downs[f]):
+            down_copy(i, f).wait_send()
 
     def wait_back(i):
         back_copy(lax.rem(me + i, ns), lax.rem(me + i, ns)).wait_recv()
+        back_copy(lax.rem(me + i, ns), me).wait_send()
 
     loop(1, ns, wait_back)
 
@@ -506,11 +537,34 @@
         g = jnp.where(tile < tpd * ns, g, 0.0)
         n, scale = normed(clips[k].astype(F32))
         v = n * gam
-        sig = 1.0 / (1.0 + jnp.exp(-v))
+        sig = 0.5 + 0.5 * jnp.tanh(0.5 * v)
         dn = g * sig * (1.0 + v * (1.0 - sig)) * gam
         gin[k] = (scale * (dn - n * jnp.mean(dn * n, axis=-1, keepdims=True))).astype(BF)
 
-    loop(0, clips.shape[0], pull, 4)
+    middle = clips.shape[0] // 2
+    loop(0, middle, pull, 4)
+
+    def wait_sp(i):
+        sp_copy(lax.rem(me + i, ns), lax.rem(me + i, ns)).wait_recv()
+
+    loop(1, ns, wait_sp)
+    finr[core, y] = jnp.sum(spr[...].astype(F32), axis=0)
+
+    def ag_copy(d, s):
+        slot = finr.at[lax.rem(s, 2), s // 2]
+        return remote(slot, slot, ag_s.at[d], ag_r.at[s], {"dp": d})
+
+    def send_ag(i):
+        ag_copy(lax.rem(dp + i, ndp), dp).start()
+
+    loop(1, ndp, send_ag)
+
+    loop(middle, clips.shape[0], pull, 4)
+
+    def done_sp(i):
+        sp_copy(lax.rem(me + i, ns), me).wait_send()
+
+    loop(1, ns, done_sp)
 
     def wait_ag(i):
         d = lax.rem(dp + i, ndp)
@@ -525,42 +579,10 @@
                 window = finr[h].reshape(ny * rc, 128)
                 fin[:, h * 128 : (h + 1) * 128] = window[off : off + wrows]
 
-    def done_space(i):
-        d = lax.rem(me + i, ns)
-        tile_copy(d, me).wait_send()
-        back_copy(d, me).wait_send()
-        sp_copy(d, me).wait_send()
-
-    loop(1, ns, done_space)
-
     def done_dp(i):
         ag_copy(lax.rem(dp + i, ndp), dp).wait_send()
 
     loop(1, ndp, done_dp)
-
-    for i in range(1, nx):
-        id_x(lax.rem(xme + i, nx), xme).wait_send()
-    for i in range(1, nz):
-        id_z(lax.rem(zme + i, nz), zme).wait_send()
-
-    def done_core(k):
-        for f in range(2):
-            core_copy(k, f).wait_send()
-
-    loop(0, ny, done_core)
-    for f in range(2):
-        for i in range(ups[f]):
-            up_copy(i, f).wait_send()
-        for i in range(downs[f]):
-            down_copy(i, f).wait_send()
-
-    @pl.when(me < ns - 1)
-    def _():
-        cot_copy.wait_send()
-
-    @pl.when(me > 0)
-    def _():
-        row_copy.wait_send()
 
 
 def pin(x):
@@ -666,6 +688,7 @@
             dma((ns,)),
             dma((2 * ny,)),
             dma((2 * ny,)),
+            pltpu.SemaphoreType.REGULAR,
         ],
         compiler_params=pltpu.CompilerParams(
             collective_id=0, has_side_effects=True, vmem_limit_bytes=48 * 1024 * 1024

time: 78.5 us -> 75 us (0.955)
  Pallas kernels: 75.6 us -> 72.1 us
    pallas_call x1, Pallas kernels: 75.6 us -> 72.1 us  [local(): pl.pallas_call(functools.partial(kernel, (ns, nx, ny, frames, half, wrows...]
where the time goes in v4:
time: 75 us; the launch traced here: 74.8 us
  Pallas kernels  72.1 us (96%)
  local copies, waits for them, and re-layouts  2.12 us (3%)
    pallas_call x1, Pallas kernels, local(): pl.pallas_call(functools.partial(kernel, (ns, nx, ny, frames, half, wrows...  72.1 us
    unnamed x3, local copies, waits for them, and re-layouts  2.12 us

profile of v4, /device:TPU:129, one launch (start us, length us, event | category | flops | bytes accessed | tf_op | source)
XLA Modules:
  0.0 74.8 jit_solution(12458554916988343634)
XLA Ops:
  0.6 72.1 %shard_map.76 = (bf16[288,256]{1,0:T(8,128)(2,1)S(1)}, bf16[32,72,128]{2,1,0:T(8,128)(2,1)S(1)}, f32[108,256]{1,0:T(8,128)S(1)}) custom-call(s32[32]{0:T(128)} %bitcast.12, s32[1,32]{1,0:T(1,128)} %ids.1, bf16[32,72,128]{2,1,0:T(8,128)(2,1)} %bitcast.10, f32[1,128]{1,0:T(1,128)} %bitcast.13, bf16[3456,256]{1,0:T(8,128)(2,1)} %weight_h.1, ...), custom_call_target="tpu_custom_call" | custom-call | tf_op jit(solution)/shard_map/pallas_call | solution.py:631
  72.7 0.7 copy.12
  73.4 0.8 %copy.13 = bf16[1,32,9,2,4,128]{5,4,3,2,1,0:T(4,128)(2,1)} copy(bf16[1,32,9,2,4,128]{5,4,3,2,1,0:T(4,128)(2,1)S(1)} %bitcast.8) | data formatting | bytes 1179648
  74.2 0.6 copy.14

commit v5 on v4

--- a/solution.py
+++ b/solution.py
@@ -271,6 +271,15 @@
         grads[2 * b + 1] = total[:, chans : 2 * chans]
 
     put_planes(back(cot, 1), 1)
+
+    def cut_tile(t, b):
+        for par in range(2):
+            for jj in range(2):
+                gtile32[t, pl.ds(b * 4 + jj * 2 + par, frames, stride=8), :] = grads[
+                    2 * b + par, pl.ds(2 * t + jj, frames, stride=half), :
+                ]
+
+    loop(0, tpd, lambda t: cut_tile(t, 1), 2)
     upper = back(cot, 0)
     gown[...] = upper
 
@@ -374,33 +383,42 @@
     up = {"dp": 2 * lax.rem(y + 1, ny) + core}
     down = {"dp": 2 * lax.rem(y + ny - 1, ny) + core}
 
-    def up_copy(i, f):
-        lo, hi = spans[f]
-        return remote(cws.at[i, lo:hi], cwr.at[i, lo:hi], cw_s.at[f, i], cw_r.at[f, i], up)
-
-    def down_copy(i, f):
-        lo, hi = spans[f]
-        return remote(ccs.at[i, lo:hi], ccr.at[i, lo:hi], cc_s.at[f, i], cc_r.at[f, i], down)
-
-    def hop(k, i, f, send, into, out_of):
-        core_copy(k, f).wait_recv()
+    def up_copy(i, f, r):
+        lo, hi, _ = flows[f][r]
+        n = sum(len(flow) for flow in flows[:f]) + r
+        return remote(cws.at[i, lo:hi], cwr.at[i, lo:hi], cw_s.at[n, i], cw_r.at[n, i], up)
+
+    def down_copy(i, f, r):
+        lo, hi, _ = flows[f][r]
+        n = sum(len(flow) for flow in flows[:f]) + r
+        return remote(ccs.at[i, lo:hi], ccr.at[i, lo:hi], cc_s.at[n, i], cc_r.at[n, i], down)
+
+    def hop(k, i, f, r, send, into, out_of):
+        lo, hi, shift = flows[f][r]
         if i > 0:
-            send(i - 1, f).wait_recv()
-
-        def add(q, s):
-            v = mine(k, q, s)
+            send(i - 1, f, r).wait_recv()
+
+        def add(q):
+            v = mine(k, q, q + shift)
             if i > 0:
                 v = v + out_of[i - 1, q].astype(F32)
             into[i, q] = v.astype(BF)
 
-        each(f, add)
-        send(i, f).start()
+        loop(lo, hi, add)
+        send(i, f, r).start()
 
     def chain(f, i):
+        k_up = lax.rem(y + ups[f] - i + ny, ny)
+        k_down = lax.rem(y + ny - downs[f] + i, ny)
         if i < ups[f]:
-            hop(lax.rem(y + ups[f] - i, ny), i, f, up_copy, cws, cwr)
+            core_copy(k_up, f).wait_recv()
         if i < downs[f]:
-            hop(lax.rem(y + ny - downs[f] + i, ny), i, f, down_copy, ccs, ccr)
+            core_copy(k_down, f).wait_recv()
+        for r in range(len(flows[f])):
+            if i < ups[f]:
+                hop(k_up, i, f, r, up_copy, cws, cwr)
+            if i < downs[f]:
+                hop(k_down, i, f, r, down_copy, ccs, ccr)
 
     weight_grad(1)
     weight_grad(0)
@@ -417,16 +435,11 @@
 
     put_planes(gown[...] + back(cotprev, 2), 0)
 
-    def cut_tile(t):
-        for b in range(2):
-            for par in range(2):
-                for jj in range(2):
-                    gtile32[t, pl.ds(b * 4 + jj * 2 + par, frames, stride=8), :] = grads[
-                        2 * b + par, pl.ds(2 * t + jj, frames, stride=half), :
-                    ]
+    def cut_upper(t):
+        cut_tile(t, 0)
         tiles[t] = gtile32[t].astype(BF)
 
-    loop(0, tpd, cut_tile, 2)
+    loop(0, tpd, cut_upper, 2)
 
     chain(0, 0)
 
@@ -452,6 +465,68 @@
     send_core(1)
     chain(0, 1)
     chain(1, 0)
+
+    for i in range(2, max(ups)):
+        chain(0, i)
+        chain(1, i - 1)
+
+    def sp_copy(d, s):
+        return remote(spst.at[d], spr.at[s], sp_s.at[d], sp_r.at[s], {"space": d})
+
+    def spread(f):
+        core_copy(y, f).wait_recv()
+        for r, (lo, hi, shift) in enumerate(flows[f]):
+            for send, steps in ((up_copy, ups), (down_copy, downs)):
+                if steps[f] > 0:
+                    send(steps[f] - 1, f, r).wait_recv()
+
+            def part(q, shift=shift):
+                s = q + shift
+                v = mine(y, q, s)
+                for landed, steps in ((cwr, ups), (ccr, downs)):
+                    if steps[f] > 0:
+                        v = v + landed[steps[f] - 1, q].astype(F32)
+                spst[s] = v.astype(BF)
+
+                @pl.when(s != me)
+                def _():
+                    sp_copy(s, me).start()
+
+            loop(lo, hi, part)
+
+    def done_tiles(i):
+        tile_copy(lax.rem(me + i, ns), me).wait_send()
+
+    loop(1, ns, done_tiles)
+    for i in range(1, nx):
+        id_x(lax.rem(xme + i, nx), xme).wait_send()
+    for i in range(1, nz):
+        id_z(lax.rem(zme + i, nz), zme).wait_send()
+
+    @pl.when(me < ns - 1)
+    def _():
+        cot_copy.wait_send()
+
+    @pl.when(me > 0)
+    def _():
+        row_copy.wait_send()
+
+    spread(0)
+    chain(1, max(ups) - 1)
+    spread(1)
+    spr[me] = spst[me]
+
+    def done_core(k):
+        for f in range(2):
+            core_copy(k, f).wait_send()
+
+    loop(0, ny, done_core)
+    for f in range(2):
+        for r in range(len(flows[f])):
+            for i in range(ups[f]):
+                up_copy(i, f, r).wait_send()
+            for i in range(downs[f]):
+                down_copy(i, f, r).wait_send()
 
     total = lax.dot_general(xmat[...], weight[18 * chans :, :], NN, preferred_element_type=F32)
     for a in (1, 0):
@@ -465,66 +540,6 @@
         total = total + jnp.concatenate([jnp.zeros((skip, 256), F32), part], axis=0)
     out[...] = total.astype(BF)
 
-
-    for i in range(2, max(ups)):
-        chain(0, i)
-        chain(1, i - 1)
-
-    def sp_copy(d, s):
-        return remote(spst.at[d], spr.at[s], sp_s.at[d], sp_r.at[s], {"space": d})
-
-    def spread(f):
-        core_copy(y, f).wait_recv()
-        for send, steps in ((up_copy, ups), (down_copy, downs)):
-            if steps[f] > 0:
-                send(steps[f] - 1, f).wait_recv()
-
-        def part(q, s):
-            v = mine(y, q, s)
-            for landed, steps in ((cwr, ups), (ccr, downs)):
-                if steps[f] > 0:
-                    v = v + landed[steps[f] - 1, q].astype(F32)
-            spst[s] = v.astype(BF)
-
-            @pl.when(s != me)
-            def _():
-                sp_copy(s, me).start()
-
-        each(f, part)
-
-    def done_tiles(i):
-        tile_copy(lax.rem(me + i, ns), me).wait_send()
-
-    loop(1, ns, done_tiles)
-    for i in range(1, nx):
-        id_x(lax.rem(xme + i, nx), xme).wait_send()
-    for i in range(1, nz):
-        id_z(lax.rem(zme + i, nz), zme).wait_send()
-
-    @pl.when(me < ns - 1)
-    def _():
-        cot_copy.wait_send()
-
-    @pl.when(me > 0)
-    def _():
-        row_copy.wait_send()
-
-    spread(0)
-    chain(1, max(ups) - 1)
-    spread(1)
-    spr[me] = spst[me]
-
-    def done_core(k):
-        for f in range(2):
-            core_copy(k, f).wait_send()
-
-    loop(0, ny, done_core)
-    for f in range(2):
-        for i in range(ups[f]):
-            up_copy(i, f).wait_send()
-        for i in range(downs[f]):
-            down_copy(i, f).wait_send()
-
     def wait_back(i):
         back_copy(lax.rem(me + i, ns), lax.rem(me + i, ns)).wait_recv()
         back_copy(lax.rem(me + i, ns), me).wait_send()
@@ -548,7 +563,7 @@
         sp_copy(lax.rem(me + i, ns), lax.rem(me + i, ns)).wait_recv()
 
     loop(1, ns, wait_sp)
-    finr[core, y] = jnp.sum(spr[...].astype(F32), axis=0)
+    finr[core, y] = jnp.sum(spr[...].astype(F32), axis=0).astype(BF)
 
     def ag_copy(d, s):
         slot = finr.at[lax.rem(s, 2), s // 2]
@@ -576,7 +591,7 @@
         @pl.when(me * wrows - begin(me) == off)
         def _(off=off):
             for h in range(2):
-                window = finr[h].reshape(ny * rc, 128)
+                window = finr[h].reshape(ny * rc, 128).astype(F32)
                 fin[:, h * 128 : (h + 1) * 128] = window[off : off + wrows]
 
     def done_dp(i):
@@ -619,6 +634,7 @@
     trows = frames * rows_in * tcols
     wrows = weight.shape[0] // ns
     nx = 4
+    ranges = sum(len(flow) for flow in flows(ns, wrows))
     rc = 16 * -(-(wrows + 12) // (16 * ny))
     pad = max(((s * wrows) // 16) * 16 + rc * ny for s in range(ns))
     vmem = pl.BlockSpec(memory_space=pltpu.VMEM)
@@ -668,7 +684,7 @@
             pltpu.VMEM((reach,) + piece, BF),
             pltpu.VMEM(piece, BF),
             pltpu.VMEM(piece, BF),
-            pltpu.VMEM((2, ny, rc, 128), F32),
+            pltpu.VMEM((2, ny, rc, 128), BF),
             dma((5,)),
             dma((nx + ns // nx,)),
             dma((nx + ns // nx,)),
@@ -680,10 +696,10 @@
             dma((2,)),
             dma((2, ny)),
             dma((2, ny)),
-            dma((2, reach)),
-            dma((2, reach)),
-            dma((2, reach)),
-            dma((2, reach)),
+            dma((ranges, reach)),
+            dma((ranges, reach)),
+            dma((ranges, reach)),
+            dma((ranges, reach)),
             dma((ns,)),
             dma((ns,)),
             dma((2 * ny,)),

time: 75 us -> 72.3 us (0.964)
  the two profiles are of different devices: /device:TPU:129 before, /device:TPU:1 now
where the time goes in v5:
time: 72.3 us; the launch traced here: 72.1 us
  Pallas kernels  69.4 us (96%)
  local copies, waits for them, and re-layouts  2.12 us (3%)
    pallas_call x1, Pallas kernels, local(): pl.pallas_call(functools.partial(kernel, (ns, nx, ny, frames, half, wrows...  69.4 us
    unnamed x3, local copies, waits for them, and re-layouts  2.12 us

profile of v5, /device:TPU:1, one launch (start us, length us, event | category | flops | bytes accessed | tf_op | source)
XLA Modules:
  0.0 72.1 jit_solution(10978741841424599169)
XLA Ops:
  0.6 69.4 %shard_map.76 = (bf16[288,256]{1,0:T(8,128)(2,1)S(1)}, bf16[32,72,128]{2,1,0:T(8,128)(2,1)S(1)}, f32[108,256]{1,0:T(8,128)S(1)}) custom-call(s32[32]{0:T(128)} %bitcast.12, s32[1,32]{1,0:T(1,128)} %ids.1, bf16[32,72,128]{2,1,0:T(8,128)(2,1)} %bitcast.10, f32[1,128]{1,0:T(1,128)} %bitcast.13, bf16[3456,256]{1,0:T(8,128)(2,1)} %weight_h.1, ...), custom_call_target="tpu_custom_call" | custom-call | tf_op jit(solution)/shard_map/pallas_call | solution.py:647
  70.0 0.7 copy.12
  70.7 0.8 %copy.13 = bf16[1,32,9,2,4,128]{5,4,3,2,1,0:T(4,128)(2,1)} copy(bf16[1,32,9,2,4,128]{5,4,3,2,1,0:T(4,128)(2,1)S(1)} %bitcast.8) | data formatting | bytes 1179648
  71.5 0.6 copy.14

commit v6 on v5

--- a/solution.py
+++ b/solution.py
@@ -232,10 +232,6 @@
 
     loop(1, ns, send_tile)
 
-    @pl.when(me < ns - 1)
-    def _():
-        cot_copy.start()
-
     @pl.when(core == 0)
     def _():
         loop(0, ny, lambda j: greet_dp(late_sem, j, 1))
@@ -304,7 +300,13 @@
     def wait_tile(i):
         tile_copy(lax.rem(me + i, ns), lax.rem(me + i, ns)).wait_recv()
 
-    loop(1, ns, wait_tile)
+    loop(1, ns // 2, wait_tile)
+
+    @pl.when(me < ns - 1)
+    def _():
+        cot_copy.start()
+
+    loop(ns // 2, ns, wait_tile)
 
     def lay_tile(t):
         tile32[t] = arr[map_s[ns, t]].astype(F32)
@@ -428,6 +430,7 @@
         pl.semaphore_wait(late_sem, ny)
 
     send_core(0)
+    chain(0, 0)
 
     @pl.when(me > 0)
     def _():
@@ -440,8 +443,6 @@
         tiles[t] = gtile32[t].astype(BF)
 
     loop(0, tpd, cut_upper, 2)
-
-    chain(0, 0)
 
     def back_copy(d, s):
         return remote(stage2.at[d], ret.at[s], rt_s.at[d], rt_r.at[s], {"space": d})
@@ -602,6 +603,15 @@
 
 def pin(x):
     return pltpu.with_memory_space_constraint(x, pltpu.HBM)
+
+
+def settle(out, gin, fin, out_to, gin_to, fin_to, sem):
+    pairs = ((out, out_to), (gin, gin_to), (fin, fin_to))
+    copies = [pltpu.make_async_copy(a, b, sem.at[i]) for i, (a, b) in enumerate(pairs)]
+    for copy in copies:
+        copy.start()
+    for copy in copies:
+        copy.wait()
 
 
 def flows(ns, wrows):
@@ -717,6 +727,14 @@
         pin(weight),
         pin(cotangent.reshape(fj, 256)),
     )
+    any_ = pl.BlockSpec(memory_space=pl.ANY)
+    out, gin, fin = pl.pallas_call(
+        settle,
+        out_shape=tuple(jax.ShapeDtypeStruct(v.shape, v.dtype) for v in (out, gin, fin)),
+        in_specs=[vmem] * 3,
+        out_specs=(any_,) * 3,
+        scratch_shapes=[dma((3,))],
+    )(*(pltpu.with_memory_space_constraint(v, pltpu.VMEM) for v in (out, gin, fin)))
     return (
         out.reshape(1, frames, 1, half, 256),
         gin.reshape(clips.shape),

time: 72.3 us -> 69.1 us (0.956)
  local copies, waits for them, and re-layouts: 2.12 us -> 0 us
  Pallas kernels: 69.4 us -> 68.2 us
    unnamed x3 -> x0, local copies, waits for them, and re-layouts: 2.12 us -> none
    pallas_call x1, Pallas kernels: 69.4 us -> 67.3 us  [local(): pl.pallas_call(functools.partial(kernel, (ns, nx, ny, frames, half, wrows...]
    pallas_call x0 -> x1, Pallas kernels: none -> 0.92 us  [local(): pl.pallas_call(settle, out_shape=tuple((jax.ShapeDtypeStruct(v.shape, v.d...]
where the time goes in v6:
time: 69.1 us; the launch traced here: 68.9 us
  Pallas kernels  68.2 us (99%)
    pallas_call x1, Pallas kernels, local(): pl.pallas_call(functools.partial(kernel, (ns, nx, ny, frames, half, wrows...  67.3 us

profile of v6, /device:TPU:1, one launch (start us, length us, event | category | flops | bytes accessed | tf_op | source)
XLA Modules:
  0.0 68.9 jit_solution(106814302982861127)
XLA Ops:
  0.6 67.3 %shard_map.76 = (bf16[288,256]{1,0:T(8,128)(2,1)S(1)}, bf16[32,72,128]{2,1,0:T(8,128)(2,1)S(1)}, f32[108,256]{1,0:T(8,128)S(1)}) custom-call(s32[32]{0:T(128)} %bitcast.10, s32[1,32]{1,0:T(1,128)} %ids.1, bf16[32,72,128]{2,1,0:T(8,128)(2,1)} %bitcast.8, f32[1,128]{1,0:T(1,128)} %bitcast.11, bf16[3456,256]{1,0:T(8,128)(2,1)} %weight_h.1, bf16[288,256]{1,0:T(8,128)(2,1)} %bitcast.9), custom_call_target="tpu_custom_call" | custom-call | tf_op jit(solution)/shard_map/pallas_call | solution.py:657
  67.9 0.9 %shard_map.77 = (bf16[288,256]{1,0:T(8,128)(2,1)}, bf16[32,72,128]{2,1,0:T(8,128)(2,1)}, f32[108,256]{1,0:T(8,128)}) custom-call(bf16[288,256]{1,0:T(8,128)(2,1)S(1)} %get-tuple-element.9.out, bf16[32,72,128]{2,1,0:T(8,128)(2,1)S(1)} %get-tuple-element.10.gin, f32[108,256]{1,0:T(8,128)S(1)} %get-tuple-element.11.fin), custom_call_target="tpu_custom_call" | custom-call | tf_op jit(solution)/shard_map/pallas_call | solution.py:731

commit v7 on v6

--- a/solution.py
+++ b/solution.py
@@ -317,7 +317,7 @@
                         t, pl.ds(b * 4 + jj * 2 + par, frames, stride=8), :
                     ]
 
-    loop(0, tpd, lay_tile, 2)
+    loop(0, tpd, lay_tile, 4)
 
     def next_col(even):
         return jnp.where(colrow == half - 1, 0.0, pltpu.roll(even, fj - 1, 0)).astype(BF)
@@ -406,7 +406,7 @@
                 v = v + out_of[i - 1, q].astype(F32)
             into[i, q] = v.astype(BF)
 
-        loop(lo, hi, add)
+        loop(lo, hi, add, hi - lo)
         send(i, f, r).start()
 
     def chain(f, i):
@@ -442,7 +442,7 @@
         cut_tile(t, 0)
         tiles[t] = gtile32[t].astype(BF)
 
-    loop(0, tpd, cut_upper, 2)
+    loop(0, tpd, cut_upper, 4)
 
     def back_copy(d, s):
         return remote(stage2.at[d], ret.at[s], rt_s.at[d], rt_r.at[s], {"space": d})

time: 69.1 us -> 68.9 us (level)
  no operation moved by 1% of the time
where the time goes in v7:
time: 68.9 us; the launch traced here: 68.5 us
  Pallas kernels  67.8 us (98%)
    pallas_call x1, Pallas kernels, local(): pl.pallas_call(functools.partial(kernel, (ns, nx, ny, frames, half, wrows...  66.9 us

profile of v7, /device:TPU:1, one launch (start us, length us, event | category | flops | bytes accessed | tf_op | source)
XLA Modules:
  0.0 68.5 jit_solution(18362216648260852145)
XLA Ops:
  0.6 66.9 %shard_map.76 = (bf16[288,256]{1,0:T(8,128)(2,1)S(1)}, bf16[32,72,128]{2,1,0:T(8,128)(2,1)S(1)}, f32[108,256]{1,0:T(8,128)S(1)}) custom-call(s32[32]{0:T(128)} %bitcast.10, s32[1,32]{1,0:T(1,128)} %ids.1, bf16[32,72,128]{2,1,0:T(8,128)(2,1)} %bitcast.8, f32[1,128]{1,0:T(1,128)} %bitcast.11, bf16[3456,256]{1,0:T(8,128)(2,1)} %weight_h.1, bf16[288,256]{1,0:T(8,128)(2,1)} %bitcast.9), custom_call_target="tpu_custom_call" | custom-call | tf_op jit(solution)/shard_map/pallas_call | solution.py:657
  67.6 0.9 %shard_map.77 = (bf16[288,256]{1,0:T(8,128)(2,1)}, bf16[32,72,128]{2,1,0:T(8,128)(2,1)}, f32[108,256]{1,0:T(8,128)}) custom-call(bf16[288,256]{1,0:T(8,128)(2,1)S(1)} %get-tuple-element.9.out, bf16[32,72,128]{2,1,0:T(8,128)(2,1)S(1)} %get-tuple-element.10.gin, f32[108,256]{1,0:T(8,128)S(1)} %get-tuple-element.11.fin), custom_call_target="tpu_custom_call" | custom-call | tf_op jit(solution)/shard_map/pallas_call | solution.py:731
